TPU v7x, 128 devices: a whole 4x4x4 slice. The times are simulated.
128 devices in a mesh: lev: 4 (over z), strip: 32 (over y, x, core).
Axes of the slice: x: 4, y: 4, z: 4, core: 2. Of those that a mesh axis runs over, the one named last changes fastest.
Arguments:
- zonal_current_grid: float32 [4, 1024, 4096], P('lev', 'strip'), may hold values from -6 to 6
- meridional_current_grid: float32 [4, 1024, 4096], P('lev', 'strip'), may hold values from -6 to 6
- thermal_anomaly: float32 [4, 1024, 4096], P('lev', 'strip'), may hold values from -6 to 6
- water_indicator: int32 [4, 1024, 4096], P('lev', 'strip'), may hold values from 0 to 1
- owner_slot_patch_number: int32 [128, 128, 8], P(('lev', 'strip')), may hold values from 0 to 511
- owner_slot_tally: int32 [128, 128], P(('lev', 'strip')), may hold values from 0 to 8, as said below
Outputs:
- samples: float32 [131072, 128], P(('lev', 'strip'))
Inputs may be any that keep to these rules, and one draw needn't show every extreme that they name: `owner_slot_patch_number`: a tile index of the source device. `owner_slot_tally`: some owner receives 8 samples from every source.
All inputs are finite; a program needn't handle non-finite values.
Results may differ from a plain program's by a relative error of at most 0.000071.
Values sent between devices are 32-bit elements; how exact they have to be, the bound alone decides.
No kernel may reach another device: no remote copies, remote signals or barrier semaphores. Data moves between devices by JAX's collectives and lax.ppermute only.
A program may use at most 64 MiB of HBM per device.

v0:
```python
import jax
import jax.numpy as jnp
from jax import lax
from jax.sharding import PartitionSpec as P

halfwidth = 20
spread_cells = 7.0
denominator_floor = 0.05


def band_weights(offsets):
    spread = offsets.astype(jnp.float32)
    tap_grid = jnp.arange(-halfwidth, halfwidth + 1).astype(jnp.float32)
    tap_total = jnp.sum(jnp.exp(-tap_grid * tap_grid / (2.0 * spread_cells * spread_cells)))
    weights = jnp.exp(-spread * spread / (2.0 * spread_cells * spread_cells)) / tap_total
    return jnp.where(jnp.abs(offsets) <= halfwidth, weights, jnp.zeros_like(weights))


def forcing_terms(filtered):
    denominator = jnp.maximum(filtered[8], denominator_floor)
    east_bar = filtered[0] / denominator
    north_bar = filtered[1] / denominator
    heat_bar = filtered[2] / denominator
    return jnp.stack(
        [
            east_bar,
            north_bar,
            heat_bar,
            filtered[3] / denominator - east_bar * east_bar,
            filtered[4] / denominator - east_bar * north_bar,
            filtered[5] / denominator - north_bar * north_bar,
            filtered[6] / denominator - east_bar * heat_bar,
            filtered[7] / denominator - north_bar * heat_bar,
        ]
    )


def zonal_filter(planes, target):
    count_planes, rows_here, width = planes.shape
    outputs_block = target.shape[1]
    blocks = planes.reshape(count_planes, rows_here, width // 128, 128)
    source = jnp.arange(128)[:, None]
    matrix = jnp.concatenate(
        [band_weights(128 * shift + source - target) for shift in (-1, 0, 1)], axis=1
    )
    mixed = jnp.einsum("prbc,cd->prbd", blocks, matrix, precision=lax.Precision.HIGHEST)
    from_before = jnp.roll(mixed[..., :outputs_block], 1, axis=2)
    own_block = mixed[..., outputs_block : 2 * outputs_block]
    from_after = jnp.roll(mixed[..., 2 * outputs_block :], -1, axis=2)
    result = from_before + own_block + from_after
    return result


def meridional_filter(item_planes):
    rows_here = item_planes.shape[1]
    strips_total = item_planes.shape[2]
    total_rows = rows_here * strips_total
    global_rows = jnp.arange(strips_total)[None, :] * rows_here + jnp.arange(rows_here)[:, None]
    rows_out = 4 * jnp.arange(total_rows // 4)[:, None, None]
    matrix = band_weights(rows_out - global_rows[None, :, :])
    return jnp.einsum("irs,prsc->pic", matrix, item_planes, precision=lax.Precision.HIGHEST)


def on_device(
    zonal_current_grid,
    meridional_current_grid,
    thermal_anomaly,
    water_indicator,
    owner_slot_patch_number,
    owner_slot_tally,
):
    zonal_current = zonal_current_grid[0]
    meridional_current = meridional_current_grid[0]
    thermal_anomaly_grid = thermal_anomaly[0]
    water_flags = water_indicator[0].astype(jnp.float32)
    planes = jnp.stack(
        [
            water_flags * zonal_current,
            water_flags * meridional_current,
            water_flags * thermal_anomaly_grid,
            water_flags * zonal_current * zonal_current,
            water_flags * zonal_current * meridional_current,
            water_flags * meridional_current * meridional_current,
            water_flags * zonal_current * thermal_anomaly_grid,
            water_flags * meridional_current * thermal_anomaly_grid,
            water_flags,
        ]
    )
    zonal_pass = zonal_filter(planes, 4 * jnp.arange(32)[None, :])
    filtered = meridional_filter(
        lax.all_to_all(zonal_pass, "strip", split_axis=2, concat_axis=2, tiled=True)
    )
    state_variables = forcing_terms(filtered)
    sampled_lat = state_variables.shape[1]
    sampled_lon = state_variables.shape[2]
    grouped = state_variables.reshape(8, sampled_lat // 4, 4, sampled_lon // 4, 4)
    tile_rows = grouped.transpose(1, 3, 0, 2, 4).reshape(-1, 128)
    ranks_total = owner_slot_patch_number.shape[1]
    capacity = owner_slot_patch_number.shape[2]
    picked = jnp.take(tile_rows, owner_slot_patch_number[0].reshape(-1), axis=0).reshape(
        ranks_total, capacity, 128
    )
    slot_index = jnp.arange(capacity)
    kept_slots = slot_index[None, :] < owner_slot_tally[0][:, None]
    outgoing = jnp.where(kept_slots[..., None], picked, jnp.zeros_like(picked))
    arrived = lax.all_to_all(outgoing, ("lev", "strip"), split_axis=0, concat_axis=0, tiled=True)
    return arrived.reshape(ranks_total * capacity, 128)


def solution(mesh):
    return jax.shard_map(
        on_device,
        mesh=mesh,
        in_specs=(
            P("lev", "strip", None),
            P("lev", "strip", None),
            P("lev", "strip", None),
            P("lev", "strip", None),
            P(("lev", "strip"), None, None),
            P(("lev", "strip"), None),
        ),
        out_specs=P(("lev", "strip"), None),
        check_vma=False,
    )
```

profile of v0, /device:TPU:1, one launch (start us, length us, event | category | flops | bytes accessed | tf_op | source)
XLA Modules:
  0.0 114.7 jit_solution(8484676661439465772)
XLA Ops:
  0.6 1.1 convert_bitcast_fusion
  1.7 2.1 %multiply_bitcast_fusion = (f32[4,8,32,128]{3,1,2,0:T(8,128)S(1)}, f32[4,8,32,128]{3,1,2,0:T(8,128)S(1)}, f32[4,8,32,128]{3,1,2,0:T(8,128)S(1)}, f32[4,8,32,128]...) fusion(f32[1,32,4096]{2,1,0:T(8,128)} %param.8, ...), kind=kLoop, calls=%fused_computation.25 | loop fusion | flops 1179648 | bytes 6291456
  5.9 4.0 %fusion.10 = f32[9,32,32,96]{3,2,1,0:T(8,128)S(1)} fusion(f32[9,32,32,128]{3,2,1,0:T(8,128)S(1)} %bitcast_dynamic-update-slice_fusion, f32[128,32]{0,1:T(8,128)S(1)} %get-tuple-element.27, f32[128,32]{0,1:T(8,128)S(1)} %get-tuple-element.26, f32[128,32]{0,1:T(8,128)S(1)} %get-tuple-element.25), kind=kOutput, calls=%fused_computation.37 | convolution fusion | flops 1358979072 | bytes 8306688 | tf_op jit(solution)/shard_map/prbc,cd->prbd/dot_general | solution.py:46
  9.9 1.8 %fusion.39 = (f32[9,32,31,32]{3,2,1,0:T(8,128)S(1)}, f32[9,32,31,32]{3,2,1,0:T(8,128)S(1)}) fusion(f32[9,32,32,96]{3,2,1,0:T(8,128)S(1)} %fusion.10), kind=kLoop, calls=%fused_computation.102 | loop fusion | bytes 4571136 | tf_op jit(solution)/shard_map/jit(_roll_static)/slice | solution.py:49
  12.2 2.4 %fusion = f32[9,32,32,32]{3,2,1,0:T(8,128)S(1)} fusion(f32[9,32,32,96]{3,2,1,0:T(8,128)S(1)} %fusion.10, f32[9,32,31,32]{3,2,1,0:T(8,128)S(1)} %get-tuple-element.11, f32[9,32,1,32]{3,2,1,0:T(1,128)S(1)} %get-tuple-element.13, f32[9,32,1,32]{3,2,1,0:T(1,128)S(1)} %get-tuple-element.12, f32[9,32,31,32]{3,2,1,0:T(8,128)S(1)} %get-tuple-element.10), kind=kLoop, calls=%fused_computation.2 | loop fusion | flops 1179648 | bytes 4718592 | tf_op jit(solution)/shard_map/add | solution.py:50
  14.6 4.9 %copy.44 = f32[9,32,32,32]{3,1,0,2:T(8,128)} copy(f32[9,32,32,32]{3,2,1,0:T(8,128)S(1)} %fusion) | data formatting | bytes 2359296 | tf_op jit(solution)/shard_map/add | solution.py:50
  19.5 5.2 %reshape.148 = f32[32,1,9216]{2,1,0:T(1,128)} reshape(f32[32,9,32,32]{3,2,1,0:T(8,128)} %bitcast.113) | data formatting | bytes 2359296
  24.7 8.6 %all-to-all-start = ((f32[32,1,9216]{2,1,0:T(1,128)}), f32[32,1,9216]{2,1,0:T(1,128)S(1)}, u32[]{:S(2)}, u32[]{:S(2)}) async-start(f32[32,1,9216]{2,1,0:T(1,128)} %reshape.148), calls=%async_computation | async-start | bytes 2359296 | tf_op jit(solution)/shard_map/all_to_all | solution.py:91
  33.8 1.2 %fusion.6 = f32[256,32,32,1]{0,2,1,3:T(8,128)S(1)} fusion(f32[]{:T(128)} %fusion.36, s32[32,32]{1,0:T(8,128)S(1)} %iota_add_fusion, s32[256]{0:T(256)S(1)} %iota_multiply_fusion), kind=kLoop, calls=%fused_computation.12 | loop fusion | flops 2359296 | bytes 1053700 | tf_op jit(solution)/shard_map/jit(_where)/select_n | solution.py:16
  34.9 16.0 %all-to-all-done = f32[32,1,9216]{2,1,0:T(1,128)S(1)} async-done(((f32[32,1,9216]{2,1,0:T(1,128)}), f32[32,1,9216]{2,1,0:T(1,128)S(1)}, u32[]{:S(2)}, u32[]{:S(2)}) %all-to-all-start) | async-done | bytes 1179680 | tf_op jit(solution)/shard_map/all_to_all | solution.py:91
  51.5 3.4 %reduce = f32[32,9216]{1,0:T(8,128)S(1)} reduce(f32[32,1,9216]{2,1,0:T(1,128)S(1)} %all-to-all-done, f32[]{:T(128)} %broadcast.130), dimensions={1}, to_apply=%all_to_all.6.reduce_sub_computation | reduce | bytes 2359300 | tf_op jit(solution)/shard_map/all_to_all | solution.py:91
  54.9 3.0 %reshape.149 = f32[32,9,32,32]{3,2,1,0:T(8,128)} reshape(f32[32,9216]{1,0:T(8,128)S(1)} %reduce) | data formatting | bytes 2359296
  57.9 10.0 %convolution_bitcast_fusion = f32[9,256,32]{1,2,0:T(8,128)S(1)} fusion(f32[256,32,32,1]{0,2,1,3:T(8,128)S(1)} %fusion.6, f32[32,9,32,32]{3,2,1,0:T(8,128)} %reshape.149), kind=kOutput, calls=%fused_computation.6 | convolution fusion | flops 905969664 | bytes 2523136 | tf_op jit(solution)/shard_map/irs,prsc->pic/dot_general | solution.py:61
  70.2 1.1 stack.69
  71.2 2.1 %stack.70 = f32[1,64,4,8,4]{2,1,4,3,0:T(8,128)} reshape(f32[1,256,32]{1,2,0:T(8,128)S(1)} %get-tuple-element.24) | data formatting | bytes 65536 | tf_op jit(solution)/shard_map/stack | solution.py:24
  73.3 1.6 %copy.21 = f32[1,64,4,8,4]{1,3,4,2,0:T(8,128)S(1)} copy(f32[1,64,4,8,4]{2,1,4,3,0:T(8,128)} %stack.70) | data formatting | bytes 65536 | tf_op jit(solution)/shard_map/stack | solution.py:24
  76.7 1.1 stack.71
  78.2 1.1 stack.72
  79.6 1.1 stack.73
  81.1 1.1 stack.74
  82.9 2.6 %copy.26 = f32[64,8,8,4,4]{1,0,4,3,2:T(8,128)} copy(f32[64,8,8,4,4]{0,1,4,3,2:T(8,128)S(1)} %bitcast.124) | data formatting | bytes 524288 | tf_op jit(solution)/shard_map/transpose | solution.py:97
  85.5 4.0 %reshape.135 = f32[512,128]{0,1:T(8,128)S(1)} reshape(f32[64,8,8,4,4]{1,0,4,3,2:T(8,128)} %copy.26) | data formatting | bytes 524288 | tf_op jit(solution)/shard_map/reshape | solution.py:97
  89.6 2.8 %gather_fusion = f32[1024,128]{1,0:T(8,128)S(1)} fusion(f32[512,128]{1,0:T(8,128)S(1)} %copy.28, s32[1024]{0:T(1024)S(1)} %broadcast_clamp_fusion), kind=kCustom, calls=%fused_computation | custom fusion | bytes 1052672 | tf_op jit(solution)/shard_map/jit(_take)/gather | solution.py:100
  92.8 21.1 %all_to_all.10 = f32[128,8,128]{2,1,0:T(8,128)S(1)} all-to-all(f32[128,8,128]{2,1,0:T(8,128)S(1)} %fusion.8), channel_id=1, replica_groups=mesh['lev'=4,'strip'=32] {'lev','strip'}, dimensions={0} | all-to-all | bytes 1048576 | tf_op jit(solution)/shard_map/all_to_all | solution.py:106
  (63 shorter events, 11.0 us)
Async XLA Ops:
  19.5 13.8 %copy-start.1 = (s32[1,128,8]{1,2,0:T(8,128)S(1)}, s32[1,128,8]{1,2,0:T(8,128)}, u32[]{:S(2)}) copy-start(s32[1,128,8]{1,2,0:T(8,128)} %param.10) | copy-start | bytes 12292
  19.5 14.2 %copy-start.2 = (s32[1,128]{1,0:T(1,128)S(1)}, s32[1,128]{1,0:T(1,128)}, u32[]{:S(2)}) copy-start(s32[1,128]{1,0:T(1,128)} %param.11) | copy-start | bytes 1540
  24.7 26.3 %all-to-all-start = ((f32[32,1,9216]{2,1,0:T(1,128)}), f32[32,1,9216]{2,1,0:T(1,128)S(1)}, u32[]{:S(2)}, u32[]{:S(2)}) async-start(f32[32,1,9216]{2,1,0:T(1,128)} %reshape.148), calls=%async_computation | async-start | bytes 2359296 | tf_op jit(solution)/shard_map/all_to_all | solution.py:91
  76.3 6.3 %copy-start = (f32[8,64,4,8,4]{1,3,4,2,0:T(8,128)S(1)}, f32[8,64,4,8,4]{1,3,4,2,0:T(8,128)}, u32[]{:S(2)}) copy-start(f32[8,64,4,8,4]{1,3,4,2,0:T(8,128)} %constant_dynamic-update-slice_fusion.7) | copy-start | bytes 786436
where the time goes:
time: 115 us
  local copies, waits for them, and re-layouts  42.4 us (37%)
  blocking collectives  21.1 us (18%)
  waiting for transfers between devices  16 us (14%)
  matrix products  14.1 us (12%)
  other arithmetic  12 us (10%)
  starting transfers between devices  8.59 us (7%)
    all_to_all x1, blocking collectives, on_device(): lax.all_to_all(outgoing, ('lev', 'strip'), split_axis=0, concat_axis=0, t...  21.1 us
    all_to_all x1, waiting for transfers between devices, on_device(): lax.all_to_all(zonal_pass, 'strip', split_axis=2, concat_axis=2, tiled=True)  16 us
    another operation x17, local copies, waits for them, and re-layouts, forcing_terms(): jnp.stack([east_bar, north_bar, heat_bar, filtered[3] / denominator - eas...  14.1 us
    unnamed x34, local copies, waits for them, and re-layouts  10.9 us
    dot_general x1, matrix products, meridional_filter(): jnp.einsum('irs,prsc->pic', matrix, item_planes, precision=lax.Precision....  10 us
    all_to_all x1, starting transfers between devices, on_device(): lax.all_to_all(zonal_pass, 'strip', split_axis=2, concat_axis=2, tiled=True)  8.59 us
    add x1, local copies, waits for them, and re-layouts, zonal_filter(): result = from_before + own_block + from_after  4.87 us
    reshape x2, local copies, waits for them, and re-layouts, on_device(): tile_rows = grouped.transpose(1, 3, 0, 2, 4).reshape(-1, 128)  4.09 us
  transfers between devices with their start and end apart: 1, of which 1 were waited for; matrix products, arithmetic and copies ran while one was open for 1% of the time, Pallas kernels for 0%

commit v1 on v0

v1 whole, which is shorter than its diff:
```python
import jax
import jax.numpy as jnp
import ml_dtypes
import numpy as np
from jax import lax
from jax.experimental import pallas as pl
from jax.experimental.pallas import tpu as pltpu
from jax.sharding import PartitionSpec as P

HALF = 20
SPREAD = 7.0
FLOOR = 0.05
ROWS = 32
COLS = 4096
STRIPS = 32
GROUPS = 5
SLAB = 48
VMEM_LIMIT = 40 * 1024 * 1024


def band(offsets):
    taps = np.arange(-HALF, HALF + 1).astype(np.float64)
    total = np.exp(-taps * taps / (2.0 * SPREAD * SPREAD)).sum()
    off = offsets.astype(np.float64)
    weights = np.exp(-off * off / (2.0 * SPREAD * SPREAD)) / total
    return np.where(np.abs(offsets) <= HALF, weights, 0.0).astype(np.float32)


def two_parts(matrix):
    high = matrix.astype(ml_dtypes.bfloat16)
    low = (matrix - high.astype(np.float32)).astype(ml_dtypes.bfloat16)
    return high, low


def zonal_matrix():
    lane = np.arange(128)
    target = ((lane // 4) % 4) * 128 + 4 * (4 * (lane // 16) + lane % 4)
    source = np.arange(768)[:, None] - 128
    return np.concatenate(two_parts(band(source - target[None, :])), axis=1)


def partial_row(a, g):
    if g < 4:
        return 4 * (g - 1) + a
    return {0: 12, 3: -5}.get(a)


def meridional_matrices():
    rows = np.arange(ROWS)
    full = np.zeros((4 * GROUPS * 8, 8 * ROWS), np.float32)
    wet = np.zeros((4 * 8, ROWS), np.float32)
    for a in range(4):
        for g in range(GROUPS):
            i = partial_row(a, g)
            if i is None:
                continue
            weights = band(4 * i - rows)
            wet[a * 8 + g] = weights
            for p in range(8):
                full[(a * GROUPS + g) * 8 + p, p * ROWS : (p + 1) * ROWS] = weights
    return np.concatenate(two_parts(full), axis=0), np.concatenate(two_parts(wet), axis=0)


def three_parts(x):
    first = x.astype(jnp.bfloat16)
    rest = x - first.astype(jnp.float32)
    second = rest.astype(jnp.bfloat16)
    third = (rest - second.astype(jnp.float32)).astype(jnp.bfloat16)
    return first, second, third


def dot(a, b):
    return jnp.dot(a, b, preferred_element_type=jnp.float32)


def swap_bit(zero, one, lane, stride):
    bit = (lane & stride) != 0
    return (
        jnp.where(bit, pltpu.roll(one, stride, 1), zero),
        jnp.where(bit, one, pltpu.roll(zero, 128 - stride, 1)),
    )


def filter_kernel(u_in, v_in, t_in, w_in, wz_ref, gm_ref, gw_ref, out_ref, ub, vb, tb, wb, parts, sems):
    order = [7, 0, 1, 2, 3, 4, 5, 6]
    copies = {}
    for c in order:
        here = pl.ds(512 * c, 512)
        for k, (src, dst) in enumerate(((u_in, ub), (v_in, vb), (t_in, tb), (w_in, wb))):
            copies[c, k] = pltpu.make_async_copy(src.at[:, here], dst.at[:, here], sems.at[k, c])
            copies[c, k].start()

    def make_planes(c):
        for k in range(4):
            copies[c, k].wait()
        for strip in range(4 * c, 4 * c + 4):
            here = slice(128 * strip, 128 * strip + 128)
            places = [slice(128 * strip + 128, 128 * strip + 256)]
            if strip == STRIPS - 1:
                places.append(slice(0, 128))
            if strip == 0:
                places.append(slice(COLS + 128, COLS + 256))
            u, v, t = ub[:, here], vb[:, here], tb[:, here]
            w = wb[:, here].astype(jnp.float32)
            wu, wv, wt = w * u, w * v, w * t
            fields = (wu, wv, wt, wu * u, wu * v, wv * v, wu * t, wv * t)
            for p, field in enumerate(fields):
                for n, part in enumerate(three_parts(field)):
                    for place in places:
                        parts[n, p * ROWS : (p + 1) * ROWS, place] = part
            for place in places:
                parts[0, 8 * ROWS : 9 * ROWS, place] = w.astype(jnp.bfloat16)

    lane = lax.broadcasted_iota(jnp.int32, (SLAB, 128), 1)

    def quad(q):
        window = slice(512 * q, 512 * q + 768)
        wz = wz_ref[...]
        z = dot(parts[1, : 8 * ROWS, window], wz)
        z = z + dot(parts[2, : 8 * ROWS, window], wz)
        z = z + dot(parts[0, : 8 * ROWS, window], wz)
        z = z[:, :128] + z[:, 128:]
        zw = dot(parts[0, 8 * ROWS :, window], wz)
        zw = zw[:, :128] + zw[:, 128:]

        def across(g_ref, x):
            m = g_ref.shape[0] // 2
            pieces = jnp.concatenate(three_parts(x), axis=1)
            y = dot(g_ref[:m], pieces)
            low = dot(g_ref[m:], pieces[:, :256])
            return (y[:, 256:] + low[:, 128:]) + (y[:, 128:256] + low[:, :128]) + y[:, :128]

        y = across(gm_ref, z)
        yw = across(gw_ref, zw)
        x = [jnp.concatenate([y[40 * a : 40 * a + 40], yw[8 * a : 8 * a + 8]], axis=0) for a in range(4)]
        x[0], x[1] = swap_bit(x[0], x[1], lane, 4)
        x[2], x[3] = swap_bit(x[2], x[3], lane, 4)
        x[0], x[2] = swap_bit(x[0], x[2], lane, 8)
        x[1], x[3] = swap_bit(x[1], x[3], lane, 8)
        for s in range(4):
            out_ref[4 * q + s] = x[s]

    make_planes(7)
    make_planes(0)
    for q in range(8):
        if q + 1 < 7:
            make_planes(q + 1)
        quad(q)


def filter_call(u, v, t, w):
    wz = zonal_matrix()
    gm, gw = meridional_matrices()
    anywhere = pl.BlockSpec(memory_space=pl.ANY)
    inside = pl.BlockSpec(memory_space=pltpu.VMEM)
    return pl.pallas_call(
        filter_kernel,
        out_shape=jax.ShapeDtypeStruct((STRIPS, SLAB, 128), jnp.float32),
        in_specs=[anywhere] * 4 + [inside] * 3,
        out_specs=inside,
        scratch_shapes=[
            pltpu.VMEM((ROWS, COLS), jnp.float32),
            pltpu.VMEM((ROWS, COLS), jnp.float32),
            pltpu.VMEM((ROWS, COLS), jnp.float32),
            pltpu.VMEM((ROWS, COLS), jnp.int32),
            pltpu.VMEM((3, 9 * ROWS, COLS + 256), jnp.bfloat16),
            pltpu.SemaphoreType.DMA((4, 8)),
        ],
        compiler_params=pltpu.CompilerParams(vmem_limit_bytes=VMEM_LIMIT),
        name="filter",
    )(u, v, t, w, jnp.asarray(wz), jnp.asarray(gm), jnp.asarray(gw))


def collect_kernel(r_ref, pick_ref, out_ref, q_scr, table):
    row = lax.broadcasted_iota(jnp.int32, (8, 128), 0)
    lane = lax.broadcasted_iota(jnp.int32, (8, 128), 1)
    a_of_lane = (lane // 4) % 4
    first_row = a_of_lane[:1] == 0
    last_row = a_of_lane[:1] == 3

    def gathered(s, half, rows_of, keep_first, keep_last):
        total = r_ref[s, rows_of(1 + half)]
        if half == 0:
            near, near_group, far, keep = s - 1, 3, s + 1, keep_last
        else:
            near, near_group, far, keep = s + 1, 0, s - 1, keep_first
        if 0 <= near < STRIPS:
            total = total + r_ref[near, rows_of(near_group)]
        if 0 <= far < STRIPS:
            total = total + jnp.where(keep, r_ref[far, rows_of(4)], 0.0)
        return total

    for s in range(STRIPS):
        for half in range(2):
            top = gathered(s, half, lambda g: slice(8 * g, 8 * g + 8), a_of_lane == 0, a_of_lane == 3)
            wet = gathered(s, half, lambda g: slice(40 + g, 41 + g), first_row, last_row)
            m = top * (1.0 / jnp.maximum(wet, FLOOR))
            u = jnp.broadcast_to(m[0:1], (8, 128))
            v = jnp.broadcast_to(m[1:2], (8, 128))
            t = jnp.broadcast_to(m[2:3], (8, 128))
            left = jnp.where(row < 3, 0.0, jnp.where((row == 5) | (row == 7), v, u))
            right = jnp.where(row == 3, u, jnp.where(row < 6, v, t))
            ti = 2 * s + half
            q_scr[8 * ti : 8 * ti + 8] = m - left * right

    for block in range(8):
        x = [q_scr[pl.ds(64 * block + q, 8, stride=8), :] for q in range(8)]
        for k in range(3):
            for i in range(8):
                if not i & (1 << k):
                    j = i | (1 << k)
                    x[i], x[j] = swap_bit(x[i], x[j], lane, 16 << k)
        rows = jnp.concatenate(x, axis=0)
        table[64 * block : 64 * block + 64] = jnp.concatenate(three_parts(rows), axis=1)

    for m in range(4):
        here = slice(256 * m, 256 * m + 256)
        picked = dot(pick_ref[here], table[...])
        out_ref[here] = (picked[:, :128] + picked[:, 128:256]) + picked[:, 256:]


def collect_call(blocks, pick):
    inside = pl.BlockSpec(memory_space=pltpu.VMEM)
    return pl.pallas_call(
        collect_kernel,
        out_shape=jax.ShapeDtypeStruct((pick.shape[0], 128), jnp.float32),
        in_specs=[inside] * 2,
        out_specs=inside,
        scratch_shapes=[
            pltpu.VMEM((512, 128), jnp.float32),
            pltpu.VMEM((512, 384), jnp.bfloat16),
        ],
        compiler_params=pltpu.CompilerParams(vmem_limit_bytes=VMEM_LIMIT),
        name="collect",
    )(blocks, pick)


def pick_matrix(patch, tally):
    ranks, capacity = patch.shape
    place = (patch // 64) * 64 + (patch % 8) * 8 + (patch // 8) % 8
    kept = jnp.arange(capacity)[None, :] < tally[:, None]
    place = jnp.where(kept, place, -1).reshape(ranks * capacity, 1)
    return (place == jnp.arange(512)[None, :]).astype(jnp.bfloat16)


def on_device(
    zonal_current_grid,
    meridional_current_grid,
    thermal_anomaly,
    water_indicator,
    owner_slot_patch_number,
    owner_slot_tally,
):
    ranks, capacity = owner_slot_patch_number.shape[1:]
    blocks = filter_call(zonal_current_grid[0], meridional_current_grid[0], thermal_anomaly[0], water_indicator[0])
    pick = pick_matrix(owner_slot_patch_number[0], owner_slot_tally[0])
    blocks = lax.all_to_all(blocks, "strip", split_axis=0, concat_axis=0, tiled=True)
    outgoing = collect_call(blocks, pick).reshape(ranks, capacity, 128)
    arrived = lax.all_to_all(outgoing, ("lev", "strip"), split_axis=0, concat_axis=0, tiled=True)
    return arrived.reshape(ranks * capacity, 128)


def solution(mesh):
    return jax.shard_map(
        on_device,
        mesh=mesh,
        in_specs=(
            P("lev", "strip", None),
            P("lev", "strip", None),
            P("lev", "strip", None),
            P("lev", "strip", None),
            P(("lev", "strip"), None, None),
            P(("lev", "strip"), None),
        ),
        out_specs=P(("lev", "strip"), None),
        check_vma=False,
    )
```

time: 115 us -> 63.6 us (0.55)
  local copies, waits for them, and re-layouts: 42.4 us -> 7.89 us
  matrix products: 14.1 us -> 0 us
  Pallas kernels: 0 us -> 12.3 us
  other arithmetic: 12 us -> 0.34 us
  waiting for transfers between devices: 16 us -> 13.6 us
    another operation x19 -> x0, local copies, waits for them, and re-layouts: 14.2 us -> none  [the longest x17 14.1 us: forcing_terms(): jnp.stack([east_bar, north_bar, heat_bar, filtered[3] / denominator - eas...]
    dot_general x2 -> x0, matrix products: 14.1 us -> none  [the longest x1 10 us: meridional_filter(): jnp.einsum('irs,prsc->pic', matrix, item_planes, precision=lax.Precision....]
    pallas_call x0 -> x2, Pallas kernels: none -> 12.3 us  [the longest x1 11.2 us: filter_call(): pl.pallas_call(filter_kernel, out_shape=jax.ShapeDtypeStruct((STRIPS, SLA...]
    add x1 -> x0, local copies, waits for them, and re-layouts: 4.87 us -> none  [zonal_filter(): result = from_before + own_block + from_after]
    reshape x2 -> x0, local copies, waits for them, and re-layouts: 4.09 us -> none  [on_device(): tile_rows = grouped.transpose(1, 3, 0, 2, 4).reshape(-1, 128)]
    all_to_all x1 -> x0, other arithmetic: 3.44 us -> none  [on_device(): lax.all_to_all(zonal_pass, 'strip', split_axis=2, concat_axis=2, tiled=True)]
    unnamed x34 -> x20, local copies, waits for them, and re-layouts: 10.9 us -> 7.7 us
    unnamed x2 -> x0, other arithmetic: 3.15 us -> none
where the time goes in v1:
time: 63.6 us; the launch traced here: 63.1 us
  blocking collectives  20.3 us (32%)
  waiting for transfers between devices  13.6 us (21%)
  Pallas kernels  12.3 us (19%)
  starting transfers between devices  8.6 us (14%)
  local copies, waits for them, and re-layouts  7.89 us (12%)
    all_to_all x1, blocking collectives, on_device(): lax.all_to_all(outgoing, ('lev', 'strip'), split_axis=0, concat_axis=0, t...  20.3 us
    all_to_all x1, waiting for transfers between devices, on_device(): lax.all_to_all(blocks, 'strip', split_axis=0, concat_axis=0, tiled=True)  13.6 us
    pallas_call x1, Pallas kernels, filter_call(): pl.pallas_call(filter_kernel, out_shape=jax.ShapeDtypeStruct((STRIPS, SLA...  11.2 us
    all_to_all x1, starting transfers between devices, on_device(): lax.all_to_all(blocks, 'strip', split_axis=0, concat_axis=0, tiled=True)  8.6 us
    unnamed x20, local copies, waits for them, and re-layouts  7.7 us
  transfers between devices with their start and end apart: 1, of which 1 were waited for; matrix products, arithmetic and copies ran while one was open for 1% of the time, Pallas kernels for 0%

profile of v1, /device:TPU:1, one launch (start us, length us, event | category | flops | bytes accessed | tf_op | source)
XLA Modules:
  0.0 63.1 jit_solution(5395295891844859322)
XLA Ops:
  0.0 1.0 %copy-done = f32[1,32,4096]{2,1,0:T(8,128)S(1)} copy-done((f32[1,32,4096]{2,1,0:T(8,128)S(1)}, f32[1,32,4096]{2,1,0:T(8,128)}, u32[]{:S(2)}) %copy-start) | copy-done | bytes 524312
  1.0 0.0 copy-start.1
  1.0 1.0 %copy-done.1 = f32[1,32,4096]{2,1,0:T(8,128)S(1)} copy-done((f32[1,32,4096]{2,1,0:T(8,128)S(1)}, f32[1,32,4096]{2,1,0:T(8,128)}, u32[]{:S(2)}) %copy-start.1) | copy-done | bytes 524312
  2.1 0.0 copy-start.2
  2.1 1.0 %copy-done.2 = f32[1,32,4096]{2,1,0:T(8,128)S(1)} copy-done((f32[1,32,4096]{2,1,0:T(8,128)S(1)}, f32[1,32,4096]{2,1,0:T(8,128)}, u32[]{:S(2)}) %copy-start.2) | copy-done | bytes 524312
  3.1 1.0 %copy-done.3 = s32[1,32,4096]{2,1,0:T(8,128)S(1)} copy-done((s32[1,32,4096]{2,1,0:T(8,128)S(1)}, s32[1,32,4096]{2,1,0:T(8,128)}, u32[]{:S(2)}) %copy-start.3) | copy-done | bytes 524312
  4.2 1.0 %copy-done.4 = bf16[768,256]{1,0:T(8,128)(2,1)S(1)} copy-done((bf16[768,256]{1,0:T(8,128)(2,1)S(1)}, bf16[768,256]{1,0:T(8,128)(2,1)}, u32[]{:S(2)}) %copy-start.4) | copy-done | bytes 393240
  5.2 0.9 %copy-done.5 = bf16[320,256]{1,0:T(8,128)(2,1)S(1)} copy-done((bf16[320,256]{1,0:T(8,128)(2,1)S(1)}, bf16[320,256]{1,0:T(8,128)(2,1)}, u32[]{:S(2)}) %copy-start.5) | copy-done | bytes 163864
  6.1 0.7 %copy-done.6 = bf16[64,32]{1,0:T(8,128)(2,1)S(1)} copy-done((bf16[64,32]{1,0:T(8,128)(2,1)S(1)}, bf16[64,32]{1,0:T(8,128)(2,1)}, u32[]{:S(2)}) %copy-start.6) | copy-done | bytes 4120
  6.8 11.2 %filter.1 = f32[32,48,128]{2,1,0:T(8,128)} custom-call(f32[32,4096]{1,0:T(8,128)S(1)} %bitcast.8, f32[32,4096]{1,0:T(8,128)S(1)} %bitcast.9, f32[32,4096]{1,0:T(8,128)S(1)} %bitcast.10, s32[32,4096]{1,0:T(8,128)S(1)} %bitcast.11, bf16[768,256]{1,0:T(8,128)(2,1)S(1)} %copy-done.4, bf16[320,256]{1,0:T(8,128)(2,1)S(1)} %copy-done.5, bf16[64,32]{1,0:T(8,128)(2,1)S(1)} %copy-done.6), custom_call_target="tpu_custom_call" | custom-call | tf_op jit(solution)/shard_map/filter/pallas_call | solution.py:156
  18.0 0.0 copy-start.8
  18.0 0.0 copy-start.7
  18.0 8.6 %all-to-all-start = ((f32[32,48,128]{2,1,0:T(8,128)}), f32[32,48,128]{2,1,0:T(8,128)S(1)}, u32[]{:S(2)}, u32[]{:S(2)}) async-start(f32[32,48,128]{2,1,0:T(8,128)} %filter.1), calls=%async_computation | async-start | bytes 1572864 | tf_op jit(solution)/shard_map/all_to_all | solution.py:257
  26.6 0.0 copy-done.8
  26.6 0.1 iota_compare_fusion.1
  26.7 0.1 lt.36
  26.8 0.0 copy-done.7
  26.8 0.1 copy.10
  26.9 0.1 squeeze.19
  27.0 0.2 fusion.pick_ref
  27.3 13.6 %all-to-all-done.r_ref = f32[32,48,128]{2,1,0:T(8,128)S(1)} async-done(((f32[32,48,128]{2,1,0:T(8,128)}), f32[32,48,128]{2,1,0:T(8,128)S(1)}, u32[]{:S(2)}, u32[]{:S(2)}) %all-to-all-start) | async-done | bytes 786464 | tf_op jit(solution)/shard_map/all_to_all | solution.py:257
  40.8 1.2 %collect.1 = f32[1024,128]{1,0:T(8,128)S(1)} custom-call(f32[32,48,128]{2,1,0:T(8,128)S(1)} %all-to-all-done.r_ref, bf16[1024,512]{1,0:T(8,128)(2,1)S(1)} %fusion.pick_ref), custom_call_target="tpu_custom_call" | custom-call | tf_op jit(solution)/shard_map/collect/pallas_call | solution.py:224
  42.0 20.3 %all_to_all.10 = f32[128,8,128]{2,1,0:T(8,128)S(1)} all-to-all(f32[128,8,128]{2,1,0:T(8,128)S(1)} %bitcast.7), channel_id=1, replica_groups=mesh['lev'=4,'strip'=32] {'lev','strip'}, dimensions={0} | all-to-all | bytes 1048576 | tf_op jit(solution)/shard_map/all_to_all | solution.py:259
  62.3 0.8 %copy.12 = f32[1024,128]{1,0:T(8,128)} copy(f32[1024,128]{1,0:T(8,128)S(1)} %bitcast.12) | data formatting | bytes 1048576
  (6 shorter events, 0.0 us)
Async XLA Ops:
  0.0 1.0 %copy-start = (f32[1,32,4096]{2,1,0:T(8,128)S(1)}, f32[1,32,4096]{2,1,0:T(8,128)}, u32[]{:S(2)}) copy-start(f32[1,32,4096]{2,1,0:T(8,128)} %param.9) | copy-start | bytes 1572868
  1.0 1.0 %copy-start.1 = (f32[1,32,4096]{2,1,0:T(8,128)S(1)}, f32[1,32,4096]{2,1,0:T(8,128)}, u32[]{:S(2)}) copy-start(f32[1,32,4096]{2,1,0:T(8,128)} %param.10) | copy-start | bytes 1572868
  2.1 1.0 %copy-start.2 = (f32[1,32,4096]{2,1,0:T(8,128)S(1)}, f32[1,32,4096]{2,1,0:T(8,128)}, u32[]{:S(2)}) copy-start(f32[1,32,4096]{2,1,0:T(8,128)} %param.11) | copy-start | bytes 1572868
  3.1 1.0 %copy-start.3 = (s32[1,32,4096]{2,1,0:T(8,128)S(1)}, s32[1,32,4096]{2,1,0:T(8,128)}, u32[]{:S(2)}) copy-start(s32[1,32,4096]{2,1,0:T(8,128)} %param.12) | copy-start | bytes 1572868
  4.2 1.0 %copy-start.4 = (bf16[768,256]{1,0:T(8,128)(2,1)S(1)}, bf16[768,256]{1,0:T(8,128)(2,1)}, u32[]{:S(2)}) copy-start(bf16[768,256]{1,0:T(8,128)(2,1)} %constant.54.clone.wz_ref) | copy-start | bytes 1179652
  5.2 0.9 %copy-start.5 = (bf16[320,256]{1,0:T(8,128)(2,1)S(1)}, bf16[320,256]{1,0:T(8,128)(2,1)}, u32[]{:S(2)}) copy-start(bf16[320,256]{1,0:T(8,128)(2,1)} %constant.55.clone.gm_ref) | copy-start | bytes 491524
  6.1 0.7 %copy-start.6 = (bf16[64,32]{1,0:T(8,128)(2,1)S(1)}, bf16[64,32]{1,0:T(8,128)(2,1)}, u32[]{:S(2)}) copy-start(bf16[64,32]{1,0:T(8,128)(2,1)} %constant.56.clone.gw_ref) | copy-start | bytes 12292
  18.0 8.6 %copy-start.8 = (s32[1,128]{1,0:T(1,128)S(1)}, s32[1,128]{1,0:T(1,128)}, u32[]{:S(2)}) copy-start(s32[1,128]{1,0:T(1,128)} %param.14) | copy-start | bytes 1540
  18.0 8.8 %copy-start.7 = (s32[1,128,8]{1,2,0:T(8,128)S(1)}, s32[1,128,8]{1,2,0:T(8,128)}, u32[]{:S(2)}) copy-start(s32[1,128,8]{1,2,0:T(8,128)} %param.13) | copy-start | bytes 12292
  18.0 22.8 %all-to-all-start = ((f32[32,48,128]{2,1,0:T(8,128)}), f32[32,48,128]{2,1,0:T(8,128)S(1)}, u32[]{:S(2)}, u32[]{:S(2)}) async-start(f32[32,48,128]{2,1,0:T(8,128)} %filter.1), calls=%async_computation | async-start | bytes 1572864 | tf_op jit(solution)/shard_map/all_to_all | solution.py:257

commit v2 on v1

--- a/solution.py
+++ b/solution.py
@@ -15,7 +15,9 @@
 STRIPS = 32
 GROUPS = 5
 SLAB = 48
-VMEM_LIMIT = 40 * 1024 * 1024
+QUADS = 8
+ENDS = (2, 8)
+VMEM_LIMIT = 62 * 1024 * 1024
 
 
 def band(offsets):
@@ -32,11 +34,14 @@
     return high, low
 
 
-def zonal_matrix():
+def zonal_matrices():
     lane = np.arange(128)
-    target = ((lane // 4) % 4) * 128 + 4 * (4 * (lane // 16) + lane % 4)
-    source = np.arange(768)[:, None] - 128
-    return np.concatenate(two_parts(band(source - target[None, :])), axis=1)
+    strip = (lane // 4) % 4
+    target = strip * 128 + 4 * (4 * (lane // 16) + lane % 4)
+    source = np.arange(256)[:, None]
+    left = band(source - np.where(strip == 3, target - 512, target)[None, :])
+    right = band(source + 256 - np.where(strip == 0, target + 512, target)[None, :])
+    return [np.concatenate(two_parts(m), axis=1) for m in (left, right)]
 
 
 def partial_row(a, g):
@@ -58,7 +63,7 @@
             wet[a * 8 + g] = weights
             for p in range(8):
                 full[(a * GROUPS + g) * 8 + p, p * ROWS : (p + 1) * ROWS] = weights
-    return np.concatenate(two_parts(full), axis=0), np.concatenate(two_parts(wet), axis=0)
+    return [np.concatenate([high] * 3 + [low], axis=1) for high, low in map(two_parts, (full, wet))]
 
 
 def three_parts(x):
@@ -81,94 +86,119 @@
     )
 
 
-def filter_kernel(u_in, v_in, t_in, w_in, wz_ref, gm_ref, gw_ref, out_ref, ub, vb, tb, wb, parts, sems):
-    order = [7, 0, 1, 2, 3, 4, 5, 6]
-    copies = {}
-    for c in order:
-        here = pl.ds(512 * c, 512)
-        for k, (src, dst) in enumerate(((u_in, ub), (v_in, vb), (t_in, tb), (w_in, wb))):
-            copies[c, k] = pltpu.make_async_copy(src.at[:, here], dst.at[:, here], sems.at[k, c])
-            copies[c, k].start()
+def filter_kernel(*refs):
+    inputs, constants, out_hbm = refs[:4], refs[4:8], refs[8]
+    held, consts, (parts, left, right, packed) = refs[9:13], refs[13:17], refs[17:21]
+    in_sems, const_sems, out_sems = refs[21:]
+    wl_ref, wr_ref, gm_ref, gw_ref = consts
+
+    loads = {}
+    starts = (0,) + ENDS[:-1]
+    for c, (begin, end) in enumerate(zip(starts, ENDS)):
+        here = pl.ds(512 * begin, 512 * (end - begin))
+        for k in range(4):
+            loads[c, k] = pltpu.make_async_copy(inputs[k].at[:, here], held[k].at[:, here], in_sems.at[k, c])
+            loads[c, k].start()
+        if c == 0:
+            fixed = [pltpu.make_async_copy(a, b, const_sems.at[n]) for n, (a, b) in enumerate(zip(constants, consts))]
+            for copy in fixed:
+                copy.start()
 
     def make_planes(c):
-        for k in range(4):
-            copies[c, k].wait()
-        for strip in range(4 * c, 4 * c + 4):
+        for strip in range(4 * starts[c], 4 * ENDS[c]):
             here = slice(128 * strip, 128 * strip + 128)
-            places = [slice(128 * strip + 128, 128 * strip + 256)]
-            if strip == STRIPS - 1:
-                places.append(slice(0, 128))
-            if strip == 0:
-                places.append(slice(COLS + 128, COLS + 256))
-            u, v, t = ub[:, here], vb[:, here], tb[:, here]
-            w = wb[:, here].astype(jnp.float32)
+            u, v, t = [held[k][:, here] for k in range(3)]
+            w = held[3][:, here].astype(jnp.float32)
             wu, wv, wt = w * u, w * v, w * t
             fields = (wu, wv, wt, wu * u, wu * v, wv * v, wu * t, wv * t)
             for p, field in enumerate(fields):
                 for n, part in enumerate(three_parts(field)):
-                    for place in places:
-                        parts[n, p * ROWS : (p + 1) * ROWS, place] = part
-            for place in places:
-                parts[0, 8 * ROWS : 9 * ROWS, place] = w.astype(jnp.bfloat16)
+                    parts[n, p * ROWS : (p + 1) * ROWS, here] = part
+            parts[0, 8 * ROWS :, here] = w.astype(jnp.bfloat16)
+
+    def zonal(q):
+        for w_ref, start, to in ((wl_ref, 0, left), (wr_ref, 256, right)):
+            window = slice(512 * q + start, 512 * q + start + 256)
+            w = w_ref[...]
+            first = dot(parts[0, :, window], w)
+            z = first[: 8 * ROWS] + dot(parts[1, : 8 * ROWS, window], w) + dot(parts[2, : 8 * ROWS, window], w)
+            to[q, : 8 * ROWS] = z[:, :128] + z[:, 128:]
+            to[q, 8 * ROWS :] = first[8 * ROWS :, :128] + first[8 * ROWS :, 128:]
 
     lane = lax.broadcasted_iota(jnp.int32, (SLAB, 128), 1)
-
-    def quad(q):
-        window = slice(512 * q, 512 * q + 768)
-        wz = wz_ref[...]
-        z = dot(parts[1, : 8 * ROWS, window], wz)
-        z = z + dot(parts[2, : 8 * ROWS, window], wz)
-        z = z + dot(parts[0, : 8 * ROWS, window], wz)
-        z = z[:, :128] + z[:, 128:]
-        zw = dot(parts[0, 8 * ROWS :, window], wz)
-        zw = zw[:, :128] + zw[:, 128:]
+    strip_of_lane = (lax.broadcasted_iota(jnp.int32, (9 * ROWS, 128), 1) // 4) % 4
+    stores = []
+
+    def meridional(pair):
+        z = []
+        for q in pair:
+            from_left = jnp.where(strip_of_lane == 3, left[(q + 1) % QUADS], left[q])
+            from_right = jnp.where(strip_of_lane == 0, right[(q - 1) % QUADS], right[q])
+            z.append(from_left + from_right)
+        z = jnp.concatenate(z, axis=1)
 
         def across(g_ref, x):
-            m = g_ref.shape[0] // 2
-            pieces = jnp.concatenate(three_parts(x), axis=1)
-            y = dot(g_ref[:m], pieces)
-            low = dot(g_ref[m:], pieces[:, :256])
-            return (y[:, 256:] + low[:, 128:]) + (y[:, 128:256] + low[:, :128]) + y[:, :128]
-
-        y = across(gm_ref, z)
-        yw = across(gw_ref, zw)
-        x = [jnp.concatenate([y[40 * a : 40 * a + 40], yw[8 * a : 8 * a + 8]], axis=0) for a in range(4)]
-        x[0], x[1] = swap_bit(x[0], x[1], lane, 4)
-        x[2], x[3] = swap_bit(x[2], x[3], lane, 4)
-        x[0], x[2] = swap_bit(x[0], x[2], lane, 8)
-        x[1], x[3] = swap_bit(x[1], x[3], lane, 8)
-        for s in range(4):
-            out_ref[4 * q + s] = x[s]
-
-    make_planes(7)
-    make_planes(0)
-    for q in range(8):
-        if q + 1 < 7:
-            make_planes(q + 1)
-        quad(q)
+            first, second, third = three_parts(x)
+            return dot(g_ref[...], jnp.concatenate([first, second, third, first], axis=0))
+
+        y = across(gm_ref, z[: 8 * ROWS])
+        yw = across(gw_ref, z[8 * ROWS :])
+        for n, q in enumerate(pair):
+            here = slice(128 * n, 128 * n + 128)
+            x = [
+                jnp.concatenate([y[40 * a : 40 * a + 40, here], yw[8 * a : 8 * a + 8, here]], axis=0)
+                for a in range(4)
+            ]
+            x[0], x[1] = swap_bit(x[0], x[1], lane, 4)
+            x[2], x[3] = swap_bit(x[2], x[3], lane, 4)
+            x[0], x[2] = swap_bit(x[0], x[2], lane, 8)
+            x[1], x[3] = swap_bit(x[1], x[3], lane, 8)
+            for s in range(4):
+                packed[4 * q + s] = x[s]
+            here = pl.ds(4 * q, 4)
+            stores.append(pltpu.make_async_copy(packed.at[here], out_hbm.at[here], out_sems.at[q]))
+            stores[-1].start()
+
+    ready = 1
+    for c, (begin, end) in enumerate(zip(starts, ENDS)):
+        for k in range(4):
+            loads[c, k].wait()
+        make_planes(c)
+        if c == 0:
+            for copy in fixed:
+                copy.wait()
+        for q in range(begin, end):
+            zonal(q)
+        while ready + 2 < end:
+            meridional((ready, ready + 1))
+            ready += 2
+    meridional((7, 0))
+    for copy in stores:
+        copy.wait()
 
 
 def filter_call(u, v, t, w):
-    wz = zonal_matrix()
-    gm, gw = meridional_matrices()
+    constants = zonal_matrices() + meridional_matrices()
     anywhere = pl.BlockSpec(memory_space=pl.ANY)
-    inside = pl.BlockSpec(memory_space=pltpu.VMEM)
     return pl.pallas_call(
         filter_kernel,
         out_shape=jax.ShapeDtypeStruct((STRIPS, SLAB, 128), jnp.float32),
-        in_specs=[anywhere] * 4 + [inside] * 3,
-        out_specs=inside,
-        scratch_shapes=[
-            pltpu.VMEM((ROWS, COLS), jnp.float32),
-            pltpu.VMEM((ROWS, COLS), jnp.float32),
-            pltpu.VMEM((ROWS, COLS), jnp.float32),
-            pltpu.VMEM((ROWS, COLS), jnp.int32),
-            pltpu.VMEM((3, 9 * ROWS, COLS + 256), jnp.bfloat16),
-            pltpu.SemaphoreType.DMA((4, 8)),
+        in_specs=[anywhere] * 8,
+        out_specs=anywhere,
+        scratch_shapes=[pltpu.VMEM((ROWS, COLS), x.dtype) for x in (u, v, t, w)]
+        + [pltpu.VMEM(x.shape, jnp.bfloat16) for x in constants]
+        + [
+            pltpu.VMEM((3, 9 * ROWS, COLS), jnp.bfloat16),
+            pltpu.VMEM((QUADS, 9 * ROWS, 128), jnp.float32),
+            pltpu.VMEM((QUADS, 9 * ROWS, 128), jnp.float32),
+            pltpu.VMEM((STRIPS, SLAB, 128), jnp.float32),
+            pltpu.SemaphoreType.DMA((4, len(ENDS))),
+            pltpu.SemaphoreType.DMA((4,)),
+            pltpu.SemaphoreType.DMA((QUADS,)),
         ],
         compiler_params=pltpu.CompilerParams(vmem_limit_bytes=VMEM_LIMIT),
         name="filter",
-    )(u, v, t, w, jnp.asarray(wz), jnp.asarray(gm), jnp.asarray(gw))
+    )(u, v, t, w, *map(jnp.asarray, constants))
 
 
 def collect_kernel(r_ref, pick_ref, out_ref, q_scr, table):

time: 63.6 us -> 54.9 us (0.86)
  local copies, waits for them, and re-layouts: 7.89 us -> 2.02 us
  Pallas kernels: 12.3 us -> 9.45 us
  waiting for transfers between devices: 13.6 us -> 12.6 us
  other arithmetic: 0.34 us -> 1.31 us
    unnamed x20 -> x8, local copies, waits for them, and re-layouts: 7.7 us -> 1.83 us
    pallas_call x1, Pallas kernels: 11.2 us -> 6.02 us  [filter_call(): pl.pallas_call(filter_kernel, out_shape=jax.ShapeDtypeStruct((STRIPS, SLA...]
    pallas_call x1, Pallas kernels: 1.17 us -> 3.43 us  [collect_call(): pl.pallas_call(collect_kernel, out_shape=jax.ShapeDtypeStruct((pick.shape...]
    convert_element_type x1, other arithmetic: 0.24 us -> 1.2 us  [pick_matrix(): return (place == jnp.arange(512)[None, :]).astype(jnp.bfloat16)]
    all_to_all x1, waiting for transfers between devices: 13.6 us -> 12.6 us  [on_device(): lax.all_to_all(blocks, 'strip', split_axis=0, concat_axis=0, tiled=True)]
  transfers between devices with their start and end apart: 1 -> 1, of which waited for: 1 -> 1; matrix products, arithmetic and copies ran while one was open for 1% -> 3% of each run, Pallas kernels for 0% -> 0%
where the time goes in v2:
time: 54.9 us; the launch traced here: 54.5 us
  blocking collectives  20.5 us (37%)
  waiting for transfers between devices  12.6 us (23%)
  Pallas kernels  9.45 us (17%)
  starting transfers between devices  8.6 us (16%)
  local copies, waits for them, and re-layouts  2.02 us (4%)
  other arithmetic  1.31 us (2%)
    all_to_all x1, blocking collectives, on_device(): lax.all_to_all(outgoing, ('lev', 'strip'), split_axis=0, concat_axis=0, t...  20.5 us
    all_to_all x1, waiting for transfers between devices, on_device(): lax.all_to_all(blocks, 'strip', split_axis=0, concat_axis=0, tiled=True)  12.6 us
    all_to_all x1, starting transfers between devices, on_device(): lax.all_to_all(blocks, 'strip', split_axis=0, concat_axis=0, tiled=True)  8.6 us
    pallas_call x1, Pallas kernels, filter_call(): pl.pallas_call(filter_kernel, out_shape=jax.ShapeDtypeStruct((STRIPS, SLA...  6.02 us
    pallas_call x1, Pallas kernels, collect_call(): pl.pallas_call(collect_kernel, out_shape=jax.ShapeDtypeStruct((pick.shape...  3.43 us
    unnamed x8, local copies, waits for them, and re-layouts  1.83 us
    convert_element_type x1, other arithmetic, pick_matrix(): return (place == jnp.arange(512)[None, :]).astype(jnp.bfloat16)  1.2 us
  transfers between devices with their start and end apart: 1, of which 1 were waited for; matrix products, arithmetic and copies ran while one was open for 3% of the time, Pallas kernels for 0%

profile of v2, /device:TPU:1, one launch (start us, length us, event | category | flops | bytes accessed | tf_op | source)
XLA Modules:
  0.0 54.5 jit_solution(1487385009378117718)
XLA Ops:
  0.0 6.0 %filter.1 = f32[32,48,128]{2,1,0:T(8,128)} custom-call(f32[32,4096]{1,0:T(8,128)} %bitcast.9, f32[32,4096]{1,0:T(8,128)} %bitcast.10, f32[32,4096]{1,0:T(8,128)} %bitcast.11, s32[32,4096]{1,0:T(8,128)} %bitcast.12, bf16[256,256]{1,0:T(8,128)(2,1)} %constant.56.clone.refs_4_, bf16[256,256]{1,0:T(8,128)(2,1)} %constant.57.clone.refs_5_, ...), custom_call_target="tpu_custom_call" | custom-call | tf_op jit(solution)/shard_map/filter/pallas_call | solution.py:183
  6.0 0.0 copy-start.2
  6.0 0.0 copy-start.1
  6.1 8.6 %all-to-all-start = ((f32[32,48,128]{2,1,0:T(8,128)}), f32[32,48,128]{2,1,0:T(8,128)S(1)}, u32[]{:S(2)}, u32[]{:S(2)}) async-start(f32[32,48,128]{2,1,0:T(8,128)} %filter.1), calls=%async_computation | async-start | bytes 1572864 | tf_op jit(solution)/shard_map/all_to_all | solution.py:287
  14.7 0.0 copy-done.2
  14.7 0.1 iota_compare_fusion.1
  14.8 0.1 lt.36
  14.9 0.0 copy-done.1
  14.9 0.1 copy.11
  15.0 0.1 squeeze.19
  15.1 1.2 %fusion.pick_ref = bf16[1024,512]{1,0:T(8,128)(2,1)} fusion(s32[1024]{0:T(1024)S(1)} %fusion.5), kind=kLoop, calls=%fused_computation.1 | loop fusion | flops 1048576 | bytes 1052672 | tf_op jit(solution)/shard_map/convert_element_type | solution.py:273
  16.3 12.6 %all-to-all-done.r_ref = f32[32,48,128]{2,1,0:T(8,128)S(1)} async-done(((f32[32,48,128]{2,1,0:T(8,128)}), f32[32,48,128]{2,1,0:T(8,128)S(1)}, u32[]{:S(2)}, u32[]{:S(2)}) %all-to-all-start) | async-done | bytes 786464 | tf_op jit(solution)/shard_map/all_to_all | solution.py:287
  28.9 0.0 copy-start
  28.9 0.9 %copy-done = f32[32,48,128]{2,1,0:T(8,128)} copy-done((f32[32,48,128]{2,1,0:T(8,128)}, f32[32,48,128]{2,1,0:T(8,128)S(1)}, u32[]{:S(2)}) %copy-start) | copy-done | bytes 786456
  29.8 3.4 %collect.1 = f32[1024,128]{1,0:T(8,128)} custom-call(f32[32,48,128]{2,1,0:T(8,128)} %copy-done, bf16[1024,512]{1,0:T(8,128)(2,1)} %fusion.pick_ref), custom_call_target="tpu_custom_call" | custom-call | tf_op jit(solution)/shard_map/collect/pallas_call | solution.py:254
  33.2 20.5 %all_to_all.10 = f32[128,8,128]{2,1,0:T(8,128)S(1)} all-to-all(f32[128,8,128]{2,1,0:T(8,128)} %bitcast.8), channel_id=1, replica_groups=mesh['lev'=4,'strip'=32] {'lev','strip'}, dimensions={0} | all-to-all | bytes 1048576 | tf_op jit(solution)/shard_map/all_to_all | solution.py:289
  53.7 0.8 %copy.13 = f32[1024,128]{1,0:T(8,128)} copy(f32[1024,128]{1,0:T(8,128)S(1)} %bitcast.7) | data formatting | bytes 1048576
  (1 shorter events, 0.0 us)
Async XLA Ops:
  6.0 8.6 %copy-start.2 = (s32[1,128]{1,0:T(1,128)S(1)}, s32[1,128]{1,0:T(1,128)}, u32[]{:S(2)}) copy-start(s32[1,128]{1,0:T(1,128)} %param.15) | copy-start | bytes 1540
  6.0 8.8 %copy-start.1 = (s32[1,128,8]{1,2,0:T(8,128)S(1)}, s32[1,128,8]{1,2,0:T(8,128)}, u32[]{:S(2)}) copy-start(s32[1,128,8]{1,2,0:T(8,128)} %param.14) | copy-start | bytes 12292
  6.1 22.8 %all-to-all-start = ((f32[32,48,128]{2,1,0:T(8,128)}), f32[32,48,128]{2,1,0:T(8,128)S(1)}, u32[]{:S(2)}, u32[]{:S(2)}) async-start(f32[32,48,128]{2,1,0:T(8,128)} %filter.1), calls=%async_computation | async-start | bytes 1572864 | tf_op jit(solution)/shard_map/all_to_all | solution.py:287
  28.9 0.9 %copy-start = (f32[32,48,128]{2,1,0:T(8,128)}, f32[32,48,128]{2,1,0:T(8,128)S(1)}, u32[]{:S(2)}) copy-start(f32[32,48,128]{2,1,0:T(8,128)S(1)} %all-to-all-done.r_ref) | copy-start | bytes 2359300

commit v3 on v2

--- a/solution.py
+++ b/solution.py
@@ -15,9 +15,12 @@
 STRIPS = 32
 GROUPS = 5
 SLAB = 48
+CHIPS = 16
+MERGED = 64
 QUADS = 8
 ENDS = (2, 8)
-VMEM_LIMIT = 62 * 1024 * 1024
+FILTER_VMEM = 24 * 1024 * 1024
+COLLECT_VMEM = 16 * 1024 * 1024
 
 
 def band(offsets):
@@ -87,9 +90,10 @@
 
 
 def filter_kernel(*refs):
-    inputs, constants, out_hbm = refs[:4], refs[4:8], refs[8]
-    held, consts, (parts, left, right, packed) = refs[9:13], refs[13:17], refs[17:21]
-    in_sems, const_sems, out_sems = refs[21:]
+    inputs, constants, outs = refs[:4], refs[4:8], refs[8:10]
+    held, consts, (parts, left, right) = refs[10:14], refs[14:18], refs[18:21]
+    in_sems, const_sems = refs[21:]
+    is_first = lax.rem(lax.axis_index("strip"), 2) == 0
     wl_ref, wr_ref, gm_ref, gw_ref = consts
 
     loads = {}
@@ -127,7 +131,6 @@
 
     lane = lax.broadcasted_iota(jnp.int32, (SLAB, 128), 1)
     strip_of_lane = (lax.broadcasted_iota(jnp.int32, (9 * ROWS, 128), 1) // 4) % 4
-    stores = []
 
     def meridional(pair):
         z = []
@@ -153,11 +156,9 @@
             x[2], x[3] = swap_bit(x[2], x[3], lane, 4)
             x[0], x[2] = swap_bit(x[0], x[2], lane, 8)
             x[1], x[3] = swap_bit(x[1], x[3], lane, 8)
-            for s in range(4):
-                packed[4 * q + s] = x[s]
-            here = pl.ds(4 * q, 4)
-            stores.append(pltpu.make_async_copy(packed.at[here], out_hbm.at[here], out_sems.at[q]))
-            stores[-1].start()
+            for n in range(2):
+                outs[0][2 * q + n] = jnp.where(is_first, x[2 * n], x[2 * n + 1])
+                outs[1][2 * q + n] = jnp.where(is_first, x[2 * n + 1], x[2 * n])
 
     ready = 1
     for c, (begin, end) in enumerate(zip(starts, ENDS)):
@@ -173,64 +174,102 @@
             meridional((ready, ready + 1))
             ready += 2
     meridional((7, 0))
-    for copy in stores:
-        copy.wait()
 
 
 def filter_call(u, v, t, w):
     constants = zonal_matrices() + meridional_matrices()
     anywhere = pl.BlockSpec(memory_space=pl.ANY)
+    u, v, t, w, *constants = [
+        pltpu.with_memory_space_constraint(jnp.asarray(x), pltpu.HBM) for x in (u, v, t, w, *constants)
+    ]
     return pl.pallas_call(
         filter_kernel,
-        out_shape=jax.ShapeDtypeStruct((STRIPS, SLAB, 128), jnp.float32),
+        out_shape=[jax.ShapeDtypeStruct((CHIPS, SLAB, 128), jnp.float32)] * 2,
         in_specs=[anywhere] * 8,
-        out_specs=anywhere,
+        out_specs=[pl.BlockSpec(memory_space=pltpu.VMEM)] * 2,
         scratch_shapes=[pltpu.VMEM((ROWS, COLS), x.dtype) for x in (u, v, t, w)]
         + [pltpu.VMEM(x.shape, jnp.bfloat16) for x in constants]
         + [
             pltpu.VMEM((3, 9 * ROWS, COLS), jnp.bfloat16),
             pltpu.VMEM((QUADS, 9 * ROWS, 128), jnp.float32),
             pltpu.VMEM((QUADS, 9 * ROWS, 128), jnp.float32),
-            pltpu.VMEM((STRIPS, SLAB, 128), jnp.float32),
             pltpu.SemaphoreType.DMA((4, len(ENDS))),
             pltpu.SemaphoreType.DMA((4,)),
-            pltpu.SemaphoreType.DMA((QUADS,)),
         ],
-        compiler_params=pltpu.CompilerParams(vmem_limit_bytes=VMEM_LIMIT),
+        compiler_params=pltpu.CompilerParams(vmem_limit_bytes=FILTER_VMEM),
         name="filter",
-    )(u, v, t, w, *map(jnp.asarray, constants))
+    )(u, v, t, w, *constants)
+
+
+def lane_rows():
+    return (lax.broadcasted_iota(jnp.int32, (8, 128), 1) // 4) % 4
+
+
+def merge_kernel(mine, theirs, out):
+    is_first = lax.rem(lax.axis_index("strip"), 2) == 0
+    a = lane_rows()
+    for chip in range(CHIPS):
+        for rows, to, keep in ((lambda g: slice(8 * g, 8 * g + 8), 0, a), (lambda g: slice(40 + g, 41 + g), 56, a[:1])):
+            x = [mine[chip, rows(g)] for g in range(GROUPS)]
+            y = [theirs[chip, rows(g)] for g in range(GROUPS)]
+            one = [jnp.where(is_first, p, q) for p, q in zip(x, y)]
+            two = [jnp.where(is_first, q, p) for p, q in zip(x, y)]
+            groups = (
+                one[0],
+                one[1] + jnp.where(keep == 3, two[4], 0.0),
+                one[2] + two[0],
+                one[3] + two[1],
+                two[2] + jnp.where(keep == 0, one[4], 0.0),
+                two[3],
+                jnp.where(keep == 3, one[4], two[4] * jnp.where(keep == 0, 1.0, 0.0)),
+            )
+            for g, group in enumerate(groups):
+                if to == 0:
+                    out[chip, 8 * g : 8 * g + 8] = group
+                else:
+                    out[chip, to + g : to + g + 1] = group
+        out[chip, MERGED - 1 : MERGED] = jnp.zeros((1, 128), jnp.float32)
+
+
+def merge_call(mine, theirs):
+    inside = pl.BlockSpec(memory_space=pltpu.VMEM)
+    return pl.pallas_call(
+        merge_kernel,
+        out_shape=jax.ShapeDtypeStruct((CHIPS, MERGED, 128), jnp.float32),
+        in_specs=[inside] * 2,
+        out_specs=inside,
+        compiler_params=pltpu.CompilerParams(vmem_limit_bytes=COLLECT_VMEM),
+        name="merge",
+    )(mine, theirs)
 
 
 def collect_kernel(r_ref, pick_ref, out_ref, q_scr, table):
     row = lax.broadcasted_iota(jnp.int32, (8, 128), 0)
     lane = lax.broadcasted_iota(jnp.int32, (8, 128), 1)
-    a_of_lane = (lane // 4) % 4
-    first_row = a_of_lane[:1] == 0
-    last_row = a_of_lane[:1] == 3
-
-    def gathered(s, half, rows_of, keep_first, keep_last):
-        total = r_ref[s, rows_of(1 + half)]
-        if half == 0:
-            near, near_group, far, keep = s - 1, 3, s + 1, keep_last
-        else:
-            near, near_group, far, keep = s + 1, 0, s - 1, keep_first
-        if 0 <= near < STRIPS:
-            total = total + r_ref[near, rows_of(near_group)]
-        if 0 <= far < STRIPS:
-            total = total + jnp.where(keep, r_ref[far, rows_of(4)], 0.0)
+    a = lane_rows()
+
+    def gathered(chip, part, rows_of, keep):
+        total = r_ref[chip, rows_of(1 + part)]
+        other = chip - 1 if part < 2 else chip + 1
+        if 0 <= other < CHIPS:
+            group = (5, 6, 6, 0)[part]
+            near = r_ref[other, rows_of(group)]
+            if group == 6:
+                near = jnp.where(keep == (0 if part == 1 else 3), near, 0.0)
+            total = total + near
         return total
 
-    for s in range(STRIPS):
-        for half in range(2):
-            top = gathered(s, half, lambda g: slice(8 * g, 8 * g + 8), a_of_lane == 0, a_of_lane == 3)
-            wet = gathered(s, half, lambda g: slice(40 + g, 41 + g), first_row, last_row)
+    for chip in range(CHIPS):
+        for part in range(4):
+            top = gathered(chip, part, lambda g: slice(8 * g, 8 * g + 8), a)
+            wet = gathered(chip, part, lambda g: slice(56 + g, 57 + g), a[:1])
             m = top * (1.0 / jnp.maximum(wet, FLOOR))
             u = jnp.broadcast_to(m[0:1], (8, 128))
             v = jnp.broadcast_to(m[1:2], (8, 128))
             t = jnp.broadcast_to(m[2:3], (8, 128))
             left = jnp.where(row < 3, 0.0, jnp.where((row == 5) | (row == 7), v, u))
             right = jnp.where(row == 3, u, jnp.where(row < 6, v, t))
-            ti = 2 * s + half
+            ti = 4 * chip + part
             q_scr[8 * ti : 8 * ti + 8] = m - left * right
 
     for block in range(8):
@@ -260,7 +299,7 @@
             pltpu.VMEM((512, 128), jnp.float32),
             pltpu.VMEM((512, 384), jnp.bfloat16),
         ],
-        compiler_params=pltpu.CompilerParams(vmem_limit_bytes=VMEM_LIMIT),
+        compiler_params=pltpu.CompilerParams(vmem_limit_bytes=COLLECT_VMEM),
         name="collect",
     )(blocks, pick)
 
@@ -282,9 +321,13 @@
     owner_slot_tally,
 ):
     ranks, capacity = owner_slot_patch_number.shape[1:]
-    blocks = filter_call(zonal_current_grid[0], meridional_current_grid[0], thermal_anomaly[0], water_indicator[0])
+    mine, theirs = filter_call(zonal_current_grid[0], meridional_current_grid[0], thermal_anomaly[0], water_indicator[0])
+    theirs = lax.ppermute(theirs, "strip", [(i, i ^ 1) for i in range(STRIPS)])
+    blocks = merge_call(mine, theirs)
     pick = pick_matrix(owner_slot_patch_number[0], owner_slot_tally[0])
-    blocks = lax.all_to_all(blocks, "strip", split_axis=0, concat_axis=0, tiled=True)
+    blocks, pick = lax.optimization_barrier((blocks, pick))
+    same_core = [list(range(core, STRIPS, 2)) for core in range(2)]
+    blocks = lax.all_to_all(blocks, "strip", split_axis=0, concat_axis=0, axis_index_groups=same_core, tiled=True)
     outgoing = collect_call(blocks, pick).reshape(ranks, capacity, 128)
     arrived = lax.all_to_all(outgoing, ("lev", "strip"), split_axis=0, concat_axis=0, tiled=True)
     return arrived.reshape(ranks * capacity, 128)

time: 54.9 us -> 49.1 us (0.89)
  blocking collectives: 20.5 us -> 38.8 us
  waiting for transfers between devices: 12.6 us -> 0.68 us
  starting transfers between devices: 8.6 us -> 1.5 us
  Pallas kernels: 9.45 us -> 6.48 us
  other arithmetic: 1.31 us -> 0.34 us
  local copies, waits for them, and re-layouts: 2.02 us -> 1.1 us
    all_to_all x0 -> x1, blocking collectives: none -> 17.4 us  [on_device(): lax.all_to_all(blocks, 'strip', split_axis=0, concat_axis=0, axis_index_g...]
    all_to_all x1 -> x0, waiting for transfers between devices: 12.6 us -> none  [on_device(): lax.all_to_all(blocks, 'strip', split_axis=0, concat_axis=0, tiled=True)]
    all_to_all x1 -> x0, starting transfers between devices: 8.6 us -> none  [on_device(): lax.all_to_all(blocks, 'strip', split_axis=0, concat_axis=0, tiled=True)]
    pallas_call x1, Pallas kernels: 3.43 us -> 1.15 us  [collect_call(): pl.pallas_call(collect_kernel, out_shape=jax.ShapeDtypeStruct((pick.shape...]
    ppermute x0 -> x1, starting transfers between devices: none -> 1.5 us  [on_device(): theirs = lax.ppermute(theirs, 'strip', [(i, i ^ 1) for i in range(STRIPS)])]
    convert_element_type x1, other arithmetic: 1.2 us -> 0.24 us  [pick_matrix(): return (place == jnp.arange(512)[None, :]).astype(jnp.bfloat16)]
    unnamed x8 -> x6, local copies, waits for them, and re-layouts: 1.83 us -> 0.9 us
    all_to_all x1, blocking collectives: 20.5 us -> 21.4 us  [on_device(): lax.all_to_all(outgoing, ('lev', 'strip'), split_axis=0, concat_axis=0, t...]
  transfers between devices with their start and end apart: 1 -> 1, of which waited for: 1 -> 1; matrix products, arithmetic and copies ran while one was open for 3% -> 1% of each run, Pallas kernels for 0% -> 0%
where the time goes in v3:
time: 49.1 us; the launch traced here: 48.9 us
  blocking collectives  38.8 us (79%)
  Pallas kernels  6.48 us (13%)
  starting transfers between devices  1.5 us (3%)
  local copies, waits for them, and re-layouts  1.1 us (2%)
  waiting for transfers between devices  0.68 us (1%)
    all_to_all x1, blocking collectives, on_device(): lax.all_to_all(outgoing, ('lev', 'strip'), split_axis=0, concat_axis=0, t...  21.4 us
    all_to_all x1, blocking collectives, on_device(): lax.all_to_all(blocks, 'strip', split_axis=0, concat_axis=0, axis_index_g...  17.4 us
    pallas_call x1, Pallas kernels, filter_call(): pl.pallas_call(filter_kernel, out_shape=[jax.ShapeDtypeStruct((CHIPS, SLA...  5.23 us
    ppermute x1, starting transfers between devices, on_device(): theirs = lax.ppermute(theirs, 'strip', [(i, i ^ 1) for i in range(STRIPS)])  1.5 us
    pallas_call x1, Pallas kernels, collect_call(): pl.pallas_call(collect_kernel, out_shape=jax.ShapeDtypeStruct((pick.shape...  1.15 us
  transfers between devices with their start and end apart: 1, of which 1 were waited for; matrix products, arithmetic and copies ran while one was open for 1% of the time, Pallas kernels for 0%

profile of v3, /device:TPU:1, one launch (start us, length us, event | category | flops | bytes accessed | tf_op | source)
XLA Modules:
  0.0 48.9 jit_solution(15890533783506660037)
XLA Ops:
  0.0 0.0 copy-start.1
  0.0 0.0 copy-start
  0.0 5.2 %filter.1 = (f32[16,48,128]{2,1,0:T(8,128)S(1)}, f32[16,48,128]{2,1,0:T(8,128)S(1)}) custom-call(f32[32,4096]{1,0:T(8,128)} %bitcast.9, f32[32,4096]{1,0:T(8,128)} %bitcast.10, f32[32,4096]{1,0:T(8,128)} %bitcast.11, s32[32,4096]{1,0:T(8,128)} %bitcast.12, bf16[256,256]{1,0:T(8,128)(2,1)} %constant.56.clone.refs_4_, ...), custom_call_target="tpu_custom_call" | custom-call | tf_op jit(solution)/shard_map/filter/pallas_call | solution.py:185
  5.2 1.5 %collective-permute-start = (f32[16,48,128]{2,1,0:T(8,128)S(1)}, f32[16,48,128]{2,1,0:T(8,128)S(1)}, u32[]{:S(2)}, u32[]{:S(2)}) collective-permute-start(f32[16,48,128]{2,1,0:T(8,128)S(1)} %get-tuple-element.10), channel_id=1, source_target_pairs={{0,1},{1,0},{2,3},{3,2},{4,5},{5,4},{6,7},{7,6},{8,9},{9,8},{10,11... | collective-permute-start | bytes 1179656 | tf_op jit(solution)/shard_map/ppermute | solution.py:325
  6.7 0.0 copy-done.1
  6.8 0.1 iota_compare_fusion.1
  6.8 0.1 lt.36
  6.9 0.0 copy-done
  7.0 0.1 copy.11
  7.1 0.1 squeeze.19
  7.2 0.2 fusion.pick_ref
  7.4 0.7 %collective-permute-done.theirs = f32[16,48,128]{2,1,0:T(8,128)S(1)} collective-permute-done((f32[16,48,128]{2,1,0:T(8,128)S(1)}, f32[16,48,128]{2,1,0:T(8,128)S(1)}, u32[]{:S(2)}, u32[]{:S(2)}) %collective-permute-start) | collective-permute-done | bytes 393248 | tf_op jit(solution)/shard_map/ppermute | solution.py:325
  8.1 0.1 merge.1
  8.2 17.4 %all_to_all.10.r_ref = f32[16,64,128]{2,1,0:T(8,128)S(1)} all-to-all(f32[16,64,128]{2,1,0:T(8,128)S(1)} %merge.1), channel_id=1, replica_groups={{0,2,4,6,8,10,12,14,16,18,20,22,24,26,28,30},{1,3,5,7,9,11,13,15,17,19,..., dimensions={0} | all-to-all | bytes 1048576 | tf_op jit(solution)/shard_map/all_to_all | solution.py:330
  25.6 1.1 %collect.1 = f32[1024,128]{1,0:T(8,128)S(1)} custom-call(f32[16,64,128]{2,1,0:T(8,128)S(1)} %all_to_all.10.r_ref, bf16[1024,512]{1,0:T(8,128)(2,1)S(1)} %fusion.pick_ref), custom_call_target="tpu_custom_call" | custom-call | tf_op jit(solution)/shard_map/collect/pallas_call | solution.py:293
  26.7 21.4 %all_to_all.11 = f32[128,8,128]{2,1,0:T(8,128)S(1)} all-to-all(f32[128,8,128]{2,1,0:T(8,128)S(1)} %bitcast.7), channel_id=1, replica_groups=mesh['lev'=4,'strip'=32] {'lev','strip'}, dimensions={0} | all-to-all | bytes 1048576 | tf_op jit(solution)/shard_map/all_to_all | solution.py:332
  48.1 0.8 %copy.13 = f32[1024,128]{1,0:T(8,128)} copy(f32[1024,128]{1,0:T(8,128)S(1)} %bitcast.8) | data formatting | bytes 1048576
  (1 shorter events, 0.0 us)
Async XLA Ops:
  0.0 6.7 %copy-start.1 = (s32[1,128]{1,0:T(1,128)S(1)}, s32[1,128]{1,0:T(1,128)}, u32[]{:S(2)}) copy-start(s32[1,128]{1,0:T(1,128)} %param.15) | copy-start | bytes 1540
  0.0 6.9 %copy-start = (s32[1,128,8]{1,2,0:T(8,128)S(1)}, s32[1,128,8]{1,2,0:T(8,128)}, u32[]{:S(2)}) copy-start(s32[1,128,8]{1,2,0:T(8,128)} %param.14) | copy-start | bytes 12292
  5.2 2.9 %collective-permute-start = (f32[16,48,128]{2,1,0:T(8,128)S(1)}, f32[16,48,128]{2,1,0:T(8,128)S(1)}, u32[]{:S(2)}, u32[]{:S(2)}) collective-permute-start(f32[16,48,128]{2,1,0:T(8,128)S(1)} %get-tuple-element.10), channel_id=1, source_target_pairs={{0,1},{1,0},{2,3},{3,2},{4,5},{5,4},{6,7},{7,6},{8,9},{9,8},{10,11... | collective-permute-start | bytes 1179656 | tf_op jit(solution)/shard_map/ppermute | solution.py:325

commit v4 on v3

--- a/solution.py
+++ b/solution.py
@@ -18,7 +18,7 @@
 CHIPS = 16
 MERGED = 64
 QUADS = 8
-ENDS = (2, 8)
+ENDS = (1, 8)
 FILTER_VMEM = 24 * 1024 * 1024
 COLLECT_VMEM = 16 * 1024 * 1024
 
@@ -66,7 +66,7 @@
             wet[a * 8 + g] = weights
             for p in range(8):
                 full[(a * GROUPS + g) * 8 + p, p * ROWS : (p + 1) * ROWS] = weights
-    return [np.concatenate([high] * 3 + [low], axis=1) for high, low in map(two_parts, (full, wet))]
+    return [np.concatenate(two_parts(m), axis=1) for m in (full, wet)]
 
 
 def three_parts(x):
@@ -116,7 +116,7 @@
             wu, wv, wt = w * u, w * v, w * t
             fields = (wu, wv, wt, wu * u, wu * v, wv * v, wu * t, wv * t)
             for p, field in enumerate(fields):
-                for n, part in enumerate(three_parts(field)):
+                for n, part in enumerate(three_parts(field)[: 3 if p < 3 else 2]):
                     parts[n, p * ROWS : (p + 1) * ROWS, here] = part
             parts[0, 8 * ROWS :, here] = w.astype(jnp.bfloat16)
 
@@ -125,8 +125,11 @@
             window = slice(512 * q + start, 512 * q + start + 256)
             w = w_ref[...]
             first = dot(parts[0, :, window], w)
-            z = first[: 8 * ROWS] + dot(parts[1, : 8 * ROWS, window], w) + dot(parts[2, : 8 * ROWS, window], w)
-            to[q, : 8 * ROWS] = z[:, :128] + z[:, 128:]
+            z = first[: 8 * ROWS] + dot(parts[1, : 8 * ROWS, window], w)
+            z = z[:, :128] + z[:, 128:]
+            third = dot(parts[2, : 3 * ROWS, window], w[:, :128])
+            to[q, : 3 * ROWS] = z[: 3 * ROWS] + third
+            to[q, 3 * ROWS : 8 * ROWS] = z[3 * ROWS :]
             to[q, 8 * ROWS :] = first[8 * ROWS :, :128] + first[8 * ROWS :, 128:]
 
     lane = lax.broadcasted_iota(jnp.int32, (SLAB, 128), 1)
@@ -142,7 +145,9 @@
 
         def across(g_ref, x):
             first, second, third = three_parts(x)
-            return dot(g_ref[...], jnp.concatenate([first, second, third, first], axis=0))
+            depth = x.shape[0]
+            high, low = g_ref[:, :depth], g_ref[:, depth:]
+            return dot(high, third) + dot(low, first) + dot(high, second) + dot(high, first)
 
         y = across(gm_ref, z[: 8 * ROWS])
         yw = across(gw_ref, z[8 * ROWS :])
@@ -280,12 +285,12 @@
                     j = i | (1 << k)
                     x[i], x[j] = swap_bit(x[i], x[j], lane, 16 << k)
         rows = jnp.concatenate(x, axis=0)
-        table[64 * block : 64 * block + 64] = jnp.concatenate(three_parts(rows), axis=1)
+        table[64 * block : 64 * block + 64] = jnp.concatenate(three_parts(rows)[:2], axis=1)
 
     for m in range(4):
         here = slice(256 * m, 256 * m + 256)
         picked = dot(pick_ref[here], table[...])
-        out_ref[here] = (picked[:, :128] + picked[:, 128:256]) + picked[:, 256:]
+        out_ref[here] = picked[:, :128] + picked[:, 128:]
 
 
 def collect_call(blocks, pick):
@@ -297,7 +302,7 @@
         out_specs=inside,
         scratch_shapes=[
             pltpu.VMEM((512, 128), jnp.float32),
-            pltpu.VMEM((512, 384), jnp.bfloat16),
+            pltpu.VMEM((512, 256), jnp.bfloat16),
         ],
         compiler_params=pltpu.CompilerParams(vmem_limit_bytes=COLLECT_VMEM),
         name="collect",

time: 49.1 us -> 48 us (0.978)
  Pallas kernels: 6.48 us -> 5.4 us
    pallas_call x1, Pallas kernels: 5.23 us -> 4.48 us  [filter_call(): pl.pallas_call(filter_kernel, out_shape=[jax.ShapeDtypeStruct((CHIPS, SLA...]
where the time goes in v4:
time: 48 us; the launch traced here: 47.8 us
  blocking collectives  38.8 us (81%)
  Pallas kernels  5.4 us (11%)
  starting transfers between devices  1.5 us (3%)
  local copies, waits for them, and re-layouts  1.1 us (2%)
  waiting for transfers between devices  0.68 us (1%)
    all_to_all x1, blocking collectives, on_device(): lax.all_to_all(outgoing, ('lev', 'strip'), split_axis=0, concat_axis=0, t...  21.4 us
    all_to_all x1, blocking collectives, on_device(): lax.all_to_all(blocks, 'strip', split_axis=0, concat_axis=0, axis_index_g...  17.4 us
    pallas_call x1, Pallas kernels, filter_call(): pl.pallas_call(filter_kernel, out_shape=[jax.ShapeDtypeStruct((CHIPS, SLA...  4.48 us
    ppermute x1, starting transfers between devices, on_device(): theirs = lax.ppermute(theirs, 'strip', [(i, i ^ 1) for i in range(STRIPS)])  1.5 us
  transfers between devices with their start and end apart: 1, of which 1 were waited for; matrix products, arithmetic and copies ran while one was open for 1% of the time, Pallas kernels for 0%

profile of v4, /device:TPU:1, one launch (start us, length us, event | category | flops | bytes accessed | tf_op | source)
XLA Modules:
  0.0 47.8 jit_solution(11215576980708954894)
XLA Ops:
  0.0 0.0 copy-start.1
  0.0 0.0 copy-start
  0.0 4.5 %filter.1 = (f32[16,48,128]{2,1,0:T(8,128)S(1)}, f32[16,48,128]{2,1,0:T(8,128)S(1)}) custom-call(f32[32,4096]{1,0:T(8,128)} %bitcast.9, f32[32,4096]{1,0:T(8,128)} %bitcast.10, f32[32,4096]{1,0:T(8,128)} %bitcast.11, s32[32,4096]{1,0:T(8,128)} %bitcast.12, bf16[256,256]{1,0:T(8,128)(2,1)} %constant.56.clone.refs_4_, ...), custom_call_target="tpu_custom_call" | custom-call | tf_op jit(solution)/shard_map/filter/pallas_call | solution.py:190
  4.5 1.5 %collective-permute-start = (f32[16,48,128]{2,1,0:T(8,128)S(1)}, f32[16,48,128]{2,1,0:T(8,128)S(1)}, u32[]{:S(2)}, u32[]{:S(2)}) collective-permute-start(f32[16,48,128]{2,1,0:T(8,128)S(1)} %get-tuple-element.10), channel_id=1, source_target_pairs={{0,1},{1,0},{2,3},{3,2},{4,5},{5,4},{6,7},{7,6},{8,9},{9,8},{10,11... | collective-permute-start | bytes 1179656 | tf_op jit(solution)/shard_map/ppermute | solution.py:330
  6.0 0.0 copy-done.1
  6.0 0.1 iota_compare_fusion.1
  6.1 0.1 lt.36
  6.2 0.0 copy-done
  6.2 0.1 copy.11
  6.3 0.1 squeeze.19
  6.4 0.2 fusion.pick_ref
  6.7 0.7 %collective-permute-done.theirs = f32[16,48,128]{2,1,0:T(8,128)S(1)} collective-permute-done((f32[16,48,128]{2,1,0:T(8,128)S(1)}, f32[16,48,128]{2,1,0:T(8,128)S(1)}, u32[]{:S(2)}, u32[]{:S(2)}) %collective-permute-start) | collective-permute-done | bytes 393248 | tf_op jit(solution)/shard_map/ppermute | solution.py:330
  7.3 0.1 merge.1
  7.4 17.4 %all_to_all.10.r_ref = f32[16,64,128]{2,1,0:T(8,128)S(1)} all-to-all(f32[16,64,128]{2,1,0:T(8,128)S(1)} %merge.1), channel_id=1, replica_groups={{0,2,4,6,8,10,12,14,16,18,20,22,24,26,28,30},{1,3,5,7,9,11,13,15,17,19,..., dimensions={0} | all-to-all | bytes 1048576 | tf_op jit(solution)/shard_map/all_to_all | solution.py:335
  24.8 0.8 %collect.1 = f32[1024,128]{1,0:T(8,128)S(1)} custom-call(f32[16,64,128]{2,1,0:T(8,128)S(1)} %all_to_all.10.r_ref, bf16[1024,512]{1,0:T(8,128)(2,1)S(1)} %fusion.pick_ref), custom_call_target="tpu_custom_call" | custom-call | tf_op jit(solution)/shard_map/collect/pallas_call | solution.py:298
  25.6 21.4 %all_to_all.11 = f32[128,8,128]{2,1,0:T(8,128)S(1)} all-to-all(f32[128,8,128]{2,1,0:T(8,128)S(1)} %bitcast.7), channel_id=1, replica_groups=mesh['lev'=4,'strip'=32] {'lev','strip'}, dimensions={0} | all-to-all | bytes 1048576 | tf_op jit(solution)/shard_map/all_to_all | solution.py:337
  47.0 0.8 %copy.13 = f32[1024,128]{1,0:T(8,128)} copy(f32[1024,128]{1,0:T(8,128)S(1)} %bitcast.8) | data formatting | bytes 1048576
  (1 shorter events, 0.0 us)
Async XLA Ops:
  0.0 6.0 %copy-start.1 = (s32[1,128]{1,0:T(1,128)S(1)}, s32[1,128]{1,0:T(1,128)}, u32[]{:S(2)}) copy-start(s32[1,128]{1,0:T(1,128)} %param.15) | copy-start | bytes 1540
  0.0 6.2 %copy-start = (s32[1,128,8]{1,2,0:T(8,128)S(1)}, s32[1,128,8]{1,2,0:T(8,128)}, u32[]{:S(2)}) copy-start(s32[1,128,8]{1,2,0:T(8,128)} %param.14) | copy-start | bytes 12292
  4.5 2.9 %collective-permute-start = (f32[16,48,128]{2,1,0:T(8,128)S(1)}, f32[16,48,128]{2,1,0:T(8,128)S(1)}, u32[]{:S(2)}, u32[]{:S(2)}) collective-permute-start(f32[16,48,128]{2,1,0:T(8,128)S(1)} %get-tuple-element.10), channel_id=1, source_target_pairs={{0,1},{1,0},{2,3},{3,2},{4,5},{5,4},{6,7},{7,6},{8,9},{9,8},{10,11... | collective-permute-start | bytes 1179656 | tf_op jit(solution)/shard_map/ppermute | solution.py:330

commit v5 on v4

--- a/solution.py
+++ b/solution.py
@@ -120,17 +120,23 @@
                     parts[n, p * ROWS : (p + 1) * ROWS, here] = part
             parts[0, 8 * ROWS :, here] = w.astype(jnp.bfloat16)
 
-    def zonal(q):
+    def zonal(quads):
         for w_ref, start, to in ((wl_ref, 0, left), (wr_ref, 256, right)):
-            window = slice(512 * q + start, 512 * q + start + 256)
             w = w_ref[...]
-            first = dot(parts[0, :, window], w)
-            z = first[: 8 * ROWS] + dot(parts[1, : 8 * ROWS, window], w)
-            z = z[:, :128] + z[:, 128:]
-            third = dot(parts[2, : 3 * ROWS, window], w[:, :128])
-            to[q, : 3 * ROWS] = z[: 3 * ROWS] + third
-            to[q, 3 * ROWS : 8 * ROWS] = z[3 * ROWS :]
-            to[q, 8 * ROWS :] = first[8 * ROWS :, :128] + first[8 * ROWS :, 128:]
+
+            def stacked(n, rows, w):
+                x = [parts[n, :rows, 512 * q + start : 512 * q + start + 256] for q in quads]
+                return dot(jnp.concatenate(x, axis=0), w).reshape(len(quads), rows, -1)
+
+            first = stacked(0, 9 * ROWS, w)
+            second = stacked(1, 8 * ROWS, w)
+            third = stacked(2, 3 * ROWS, w[:, :128])
+            for n, q in enumerate(quads):
+                z = first[n, : 8 * ROWS] + second[n]
+                z = z[:, :128] + z[:, 128:]
+                to[q, : 3 * ROWS] = z[: 3 * ROWS] + third[n]
+                to[q, 3 * ROWS : 8 * ROWS] = z[3 * ROWS :]
+                to[q, 8 * ROWS :] = first[n, 8 * ROWS :, :128] + first[n, 8 * ROWS :, 128:]
 
     lane = lax.broadcasted_iota(jnp.int32, (SLAB, 128), 1)
     strip_of_lane = (lax.broadcasted_iota(jnp.int32, (9 * ROWS, 128), 1) // 4) % 4
@@ -173,8 +179,8 @@
         if c == 0:
             for copy in fixed:
                 copy.wait()
-        for q in range(begin, end):
-            zonal(q)
+        for q in range(begin, end, 4):
+            zonal(range(q, min(q + 4, end)))
         while ready + 2 < end:
             meridional((ready, ready + 1))
             ready += 2

time: 48 us -> 47.9 us (level)
  no operation moved by 1% of the time
where the time goes in v5:
time: 47.9 us; the launch traced here: 47.7 us
  blocking collectives  38.8 us (81%)
  Pallas kernels  5.28 us (11%)
  starting transfers between devices  1.5 us (3%)
  local copies, waits for them, and re-layouts  1.1 us (2%)
  waiting for transfers between devices  0.68 us (1%)
    all_to_all x1, blocking collectives, on_device(): lax.all_to_all(outgoing, ('lev', 'strip'), split_axis=0, concat_axis=0, t...  21.4 us
    all_to_all x1, blocking collectives, on_device(): lax.all_to_all(blocks, 'strip', split_axis=0, concat_axis=0, axis_index_g...  17.4 us
    pallas_call x1, Pallas kernels, filter_call(): pl.pallas_call(filter_kernel, out_shape=[jax.ShapeDtypeStruct((CHIPS, SLA...  4.37 us
    ppermute x1, starting transfers between devices, on_device(): theirs = lax.ppermute(theirs, 'strip', [(i, i ^ 1) for i in range(STRIPS)])  1.5 us
  transfers between devices with their start and end apart: 1, of which 1 were waited for; matrix products, arithmetic and copies ran while one was open for 1% of the time, Pallas kernels for 0%

profile of v5, /device:TPU:1, one launch (start us, length us, event | category | flops | bytes accessed | tf_op | source)
XLA Modules:
  0.0 47.7 jit_solution(625470239626841133)
XLA Ops:
  0.0 0.0 copy-start.1
  0.0 0.0 copy-start
  0.0 4.4 %filter.1 = (f32[16,48,128]{2,1,0:T(8,128)S(1)}, f32[16,48,128]{2,1,0:T(8,128)S(1)}) custom-call(f32[32,4096]{1,0:T(8,128)} %bitcast.9, f32[32,4096]{1,0:T(8,128)} %bitcast.10, f32[32,4096]{1,0:T(8,128)} %bitcast.11, s32[32,4096]{1,0:T(8,128)} %bitcast.12, bf16[256,256]{1,0:T(8,128)(2,1)} %constant.56.clone.refs_4_, ...), custom_call_target="tpu_custom_call" | custom-call | tf_op jit(solution)/shard_map/filter/pallas_call | solution.py:196
  4.4 1.5 %collective-permute-start = (f32[16,48,128]{2,1,0:T(8,128)S(1)}, f32[16,48,128]{2,1,0:T(8,128)S(1)}, u32[]{:S(2)}, u32[]{:S(2)}) collective-permute-start(f32[16,48,128]{2,1,0:T(8,128)S(1)} %get-tuple-element.10), channel_id=1, source_target_pairs={{0,1},{1,0},{2,3},{3,2},{4,5},{5,4},{6,7},{7,6},{8,9},{9,8},{10,11... | collective-permute-start | bytes 1179656 | tf_op jit(solution)/shard_map/ppermute | solution.py:336
  5.9 0.0 copy-done.1
  5.9 0.1 iota_compare_fusion.1
  6.0 0.1 lt.36
  6.1 0.0 copy-done
  6.1 0.1 copy.11
  6.2 0.1 squeeze.19
  6.3 0.2 fusion.pick_ref
  6.5 0.7 %collective-permute-done.theirs = f32[16,48,128]{2,1,0:T(8,128)S(1)} collective-permute-done((f32[16,48,128]{2,1,0:T(8,128)S(1)}, f32[16,48,128]{2,1,0:T(8,128)S(1)}, u32[]{:S(2)}, u32[]{:S(2)}) %collective-permute-start) | collective-permute-done | bytes 393248 | tf_op jit(solution)/shard_map/ppermute | solution.py:336
  7.2 0.1 merge.1
  7.3 17.4 %all_to_all.10.r_ref = f32[16,64,128]{2,1,0:T(8,128)S(1)} all-to-all(f32[16,64,128]{2,1,0:T(8,128)S(1)} %merge.1), channel_id=1, replica_groups={{0,2,4,6,8,10,12,14,16,18,20,22,24,26,28,30},{1,3,5,7,9,11,13,15,17,19,..., dimensions={0} | all-to-all | bytes 1048576 | tf_op jit(solution)/shard_map/all_to_all | solution.py:341
  24.7 0.8 %collect.1 = f32[1024,128]{1,0:T(8,128)S(1)} custom-call(f32[16,64,128]{2,1,0:T(8,128)S(1)} %all_to_all.10.r_ref, bf16[1024,512]{1,0:T(8,128)(2,1)S(1)} %fusion.pick_ref), custom_call_target="tpu_custom_call" | custom-call | tf_op jit(solution)/shard_map/collect/pallas_call | solution.py:304
  25.5 21.4 %all_to_all.11 = f32[128,8,128]{2,1,0:T(8,128)S(1)} all-to-all(f32[128,8,128]{2,1,0:T(8,128)S(1)} %bitcast.7), channel_id=1, replica_groups=mesh['lev'=4,'strip'=32] {'lev','strip'}, dimensions={0} | all-to-all | bytes 1048576 | tf_op jit(solution)/shard_map/all_to_all | solution.py:343
  46.9 0.8 %copy.13 = f32[1024,128]{1,0:T(8,128)} copy(f32[1024,128]{1,0:T(8,128)S(1)} %bitcast.8) | data formatting | bytes 1048576
  (1 shorter events, 0.0 us)
Async XLA Ops:
  0.0 5.9 %copy-start.1 = (s32[1,128]{1,0:T(1,128)S(1)}, s32[1,128]{1,0:T(1,128)}, u32[]{:S(2)}) copy-start(s32[1,128]{1,0:T(1,128)} %param.15) | copy-start | bytes 1540
  0.0 6.1 %copy-start = (s32[1,128,8]{1,2,0:T(8,128)S(1)}, s32[1,128,8]{1,2,0:T(8,128)}, u32[]{:S(2)}) copy-start(s32[1,128,8]{1,2,0:T(8,128)} %param.14) | copy-start | bytes 12292
  4.4 2.9 %collective-permute-start = (f32[16,48,128]{2,1,0:T(8,128)S(1)}, f32[16,48,128]{2,1,0:T(8,128)S(1)}, u32[]{:S(2)}, u32[]{:S(2)}) collective-permute-start(f32[16,48,128]{2,1,0:T(8,128)S(1)} %get-tuple-element.10), channel_id=1, source_target_pairs={{0,1},{1,0},{2,3},{3,2},{4,5},{5,4},{6,7},{7,6},{8,9},{9,8},{10,11... | collective-permute-start | bytes 1179656 | tf_op jit(solution)/shard_map/ppermute | solution.py:336

commit v6 on v5

--- a/solution.py
+++ b/solution.py
@@ -16,6 +16,8 @@
 GROUPS = 5
 SLAB = 48
 CHIPS = 16
+ORDER = [4 * y + (x if y % 2 == 0 else 3 - x) for y in range(4) for x in range(4)]
+PLACE = [ORDER.index(chip) for chip in range(CHIPS)]
 MERGED = 64
 QUADS = 8
 ENDS = (1, 8)
@@ -236,10 +238,10 @@
             )
             for g, group in enumerate(groups):
                 if to == 0:
-                    out[chip, 8 * g : 8 * g + 8] = group
+                    out[PLACE[chip], 8 * g : 8 * g + 8] = group
                 else:
-                    out[chip, to + g : to + g + 1] = group
-        out[chip, MERGED - 1 : MERGED] = jnp.zeros((1, 128), jnp.float32)
+                    out[PLACE[chip], to + g : to + g + 1] = group
+        out[PLACE[chip], MERGED - 1 : MERGED] = jnp.zeros((1, 128), jnp.float32)
 
 
 def merge_call(mine, theirs):
@@ -260,11 +262,11 @@
     a = lane_rows()
 
     def gathered(chip, part, rows_of, keep):
-        total = r_ref[chip, rows_of(1 + part)]
+        total = r_ref[PLACE[chip], rows_of(1 + part)]
         other = chip - 1 if part < 2 else chip + 1
         if 0 <= other < CHIPS:
             group = (5, 6, 6, 0)[part]
-            near = r_ref[other, rows_of(group)]
+            near = r_ref[PLACE[other], rows_of(group)]
             if group == 6:
                 near = jnp.where(keep == (0 if part == 1 else 3), near, 0.0)
             total = total + near
@@ -337,7 +339,7 @@
     blocks = merge_call(mine, theirs)
     pick = pick_matrix(owner_slot_patch_number[0], owner_slot_tally[0])
     blocks, pick = lax.optimization_barrier((blocks, pick))
-    same_core = [list(range(core, STRIPS, 2)) for core in range(2)]
+    same_core = [[2 * chip + core for chip in ORDER] for core in range(2)]
     blocks = lax.all_to_all(blocks, "strip", split_axis=0, concat_axis=0, axis_index_groups=same_core, tiled=True)
     outgoing = collect_call(blocks, pick).reshape(ranks, capacity, 128)
     arrived = lax.all_to_all(outgoing, ("lev", "strip"), split_axis=0, concat_axis=0, tiled=True)

time: 47.9 us -> 47.8 us (level)
    all_to_all x1, blocking collectives: 17.4 us -> 16.1 us  [on_device(): lax.all_to_all(blocks, 'strip', split_axis=0, concat_axis=0, axis_index_g...]
    all_to_all x1, blocking collectives: 21.4 us -> 22.6 us  [on_device(): lax.all_to_all(outgoing, ('lev', 'strip'), split_axis=0, concat_axis=0, t...]
where the time goes in v6:
time: 47.8 us; the launch traced here: 47.6 us
  blocking collectives  38.7 us (81%)
  Pallas kernels  5.28 us (11%)
  starting transfers between devices  1.5 us (3%)
  local copies, waits for them, and re-layouts  1.1 us (2%)
  waiting for transfers between devices  0.68 us (1%)
    all_to_all x1, blocking collectives, on_device(): lax.all_to_all(outgoing, ('lev', 'strip'), split_axis=0, concat_axis=0, t...  22.6 us
    all_to_all x1, blocking collectives, on_device(): lax.all_to_all(blocks, 'strip', split_axis=0, concat_axis=0, axis_index_g...  16.1 us
    pallas_call x1, Pallas kernels, filter_call(): pl.pallas_call(filter_kernel, out_shape=[jax.ShapeDtypeStruct((CHIPS, SLA...  4.37 us
    ppermute x1, starting transfers between devices, on_device(): theirs = lax.ppermute(theirs, 'strip', [(i, i ^ 1) for i in range(STRIPS)])  1.5 us
  transfers between devices with their start and end apart: 1, of which 1 were waited for; matrix products, arithmetic and copies ran while one was open for 1% of the time, Pallas kernels for 0%

profile of v6, /device:TPU:1, one launch (start us, length us, event | category | flops | bytes accessed | tf_op | source)
XLA Modules:
  0.0 47.6 jit_solution(12158796852874106695)
XLA Ops:
  0.0 0.0 copy-start.1
  0.0 0.0 copy-start
  0.0 4.4 %filter.1 = (f32[16,48,128]{2,1,0:T(8,128)S(1)}, f32[16,48,128]{2,1,0:T(8,128)S(1)}) custom-call(f32[32,4096]{1,0:T(8,128)} %bitcast.9, f32[32,4096]{1,0:T(8,128)} %bitcast.10, f32[32,4096]{1,0:T(8,128)} %bitcast.11, s32[32,4096]{1,0:T(8,128)} %bitcast.12, bf16[256,256]{1,0:T(8,128)(2,1)} %constant.56.clone.refs_4_, ...), custom_call_target="tpu_custom_call" | custom-call | tf_op jit(solution)/shard_map/filter/pallas_call | solution.py:198
  4.4 1.5 %collective-permute-start = (f32[16,48,128]{2,1,0:T(8,128)S(1)}, f32[16,48,128]{2,1,0:T(8,128)S(1)}, u32[]{:S(2)}, u32[]{:S(2)}) collective-permute-start(f32[16,48,128]{2,1,0:T(8,128)S(1)} %get-tuple-element.10), channel_id=1, source_target_pairs={{0,1},{1,0},{2,3},{3,2},{4,5},{5,4},{6,7},{7,6},{8,9},{9,8},{10,11... | collective-permute-start | bytes 1179656 | tf_op jit(solution)/shard_map/ppermute | solution.py:338
  5.9 0.0 copy-done.1
  5.9 0.1 iota_compare_fusion.1
  6.0 0.1 lt.36
  6.1 0.0 copy-done
  6.1 0.1 copy.11
  6.2 0.1 squeeze.19
  6.3 0.2 fusion.pick_ref
  6.5 0.7 %collective-permute-done.theirs = f32[16,48,128]{2,1,0:T(8,128)S(1)} collective-permute-done((f32[16,48,128]{2,1,0:T(8,128)S(1)}, f32[16,48,128]{2,1,0:T(8,128)S(1)}, u32[]{:S(2)}, u32[]{:S(2)}) %collective-permute-start) | collective-permute-done | bytes 393248 | tf_op jit(solution)/shard_map/ppermute | solution.py:338
  7.2 0.1 merge.1
  7.3 16.1 %all_to_all.10.r_ref = f32[16,64,128]{2,1,0:T(8,128)S(1)} all-to-all(f32[16,64,128]{2,1,0:T(8,128)S(1)} %merge.1), channel_id=1, replica_groups={{0,2,4,6,14,12,10,8,16,18,20,22,30,28,26,24},{1,3,5,7,15,13,11,9,17,19,..., dimensions={0} | all-to-all | bytes 1048576 | tf_op jit(solution)/shard_map/all_to_all | solution.py:343
  23.4 0.8 %collect.1 = f32[1024,128]{1,0:T(8,128)S(1)} custom-call(f32[16,64,128]{2,1,0:T(8,128)S(1)} %all_to_all.10.r_ref, bf16[1024,512]{1,0:T(8,128)(2,1)S(1)} %fusion.pick_ref), custom_call_target="tpu_custom_call" | custom-call | tf_op jit(solution)/shard_map/collect/pallas_call | solution.py:306
  24.2 22.6 %all_to_all.11 = f32[128,8,128]{2,1,0:T(8,128)S(1)} all-to-all(f32[128,8,128]{2,1,0:T(8,128)S(1)} %bitcast.7), channel_id=1, replica_groups=mesh['lev'=4,'strip'=32] {'lev','strip'}, dimensions={0} | all-to-all | bytes 1048576 | tf_op jit(solution)/shard_map/all_to_all | solution.py:345
  46.8 0.8 %copy.13 = f32[1024,128]{1,0:T(8,128)} copy(f32[1024,128]{1,0:T(8,128)S(1)} %bitcast.8) | data formatting | bytes 1048576
  (1 shorter events, 0.0 us)
Async XLA Ops:
  0.0 5.9 %copy-start.1 = (s32[1,128]{1,0:T(1,128)S(1)}, s32[1,128]{1,0:T(1,128)}, u32[]{:S(2)}) copy-start(s32[1,128]{1,0:T(1,128)} %param.15) | copy-start | bytes 1540
  0.0 6.1 %copy-start = (s32[1,128,8]{1,2,0:T(8,128)S(1)}, s32[1,128,8]{1,2,0:T(8,128)}, u32[]{:S(2)}) copy-start(s32[1,128,8]{1,2,0:T(8,128)} %param.14) | copy-start | bytes 12292
  4.4 2.9 %collective-permute-start = (f32[16,48,128]{2,1,0:T(8,128)S(1)}, f32[16,48,128]{2,1,0:T(8,128)S(1)}, u32[]{:S(2)}, u32[]{:S(2)}) collective-permute-start(f32[16,48,128]{2,1,0:T(8,128)S(1)} %get-tuple-element.10), channel_id=1, source_target_pairs={{0,1},{1,0},{2,3},{3,2},{4,5},{5,4},{6,7},{7,6},{8,9},{9,8},{10,11... | collective-permute-start | bytes 1179656 | tf_op jit(solution)/shard_map/ppermute | solution.py:338

commit v7 on v5

--- a/solution.py
+++ b/solution.py
@@ -18,7 +18,7 @@
 CHIPS = 16
 MERGED = 64
 QUADS = 8
-ENDS = (1, 8)
+ENDS = (2, 8)
 FILTER_VMEM = 24 * 1024 * 1024
 COLLECT_VMEM = 16 * 1024 * 1024
 
@@ -179,8 +179,8 @@
         if c == 0:
             for copy in fixed:
                 copy.wait()
-        for q in range(begin, end, 4):
-            zonal(range(q, min(q + 4, end)))
+        for q in range(begin, end, 3):
+            zonal(range(q, min(q + 3, end)))
         while ready + 2 < end:
             meridional((ready, ready + 1))
             ready += 2

time: 47.9 us -> 48 us (level)
  no operation moved by 1% of the time
where the time goes in v7:
time: 48 us; the launch traced here: 47.8 us
  blocking collectives  38.8 us (81%)
  Pallas kernels  5.37 us (11%)
  starting transfers between devices  1.5 us (3%)
  local copies, waits for them, and re-layouts  1.1 us (2%)
  waiting for transfers between devices  0.68 us (1%)
    all_to_all x1, blocking collectives, on_device(): lax.all_to_all(outgoing, ('lev', 'strip'), split_axis=0, concat_axis=0, t...  21.4 us
    all_to_all x1, blocking collectives, on_device(): lax.all_to_all(blocks, 'strip', split_axis=0, concat_axis=0, axis_index_g...  17.4 us
    pallas_call x1, Pallas kernels, filter_call(): pl.pallas_call(filter_kernel, out_shape=[jax.ShapeDtypeStruct((CHIPS, SLA...  4.45 us
    ppermute x1, starting transfers between devices, on_device(): theirs = lax.ppermute(theirs, 'strip', [(i, i ^ 1) for i in range(STRIPS)])  1.5 us
  transfers between devices with their start and end apart: 1, of which 1 were waited for; matrix products, arithmetic and copies ran while one was open for 1% of the time, Pallas kernels for 0%

profile of v7, /device:TPU:1, one launch (start us, length us, event | category | flops | bytes accessed | tf_op | source)
XLA Modules:
  0.0 47.8 jit_solution(12406103094465177176)
XLA Ops:
  0.0 0.0 copy-start.1
  0.0 0.0 copy-start
  0.0 4.5 %filter.1 = (f32[16,48,128]{2,1,0:T(8,128)S(1)}, f32[16,48,128]{2,1,0:T(8,128)S(1)}) custom-call(f32[32,4096]{1,0:T(8,128)} %bitcast.9, f32[32,4096]{1,0:T(8,128)} %bitcast.10, f32[32,4096]{1,0:T(8,128)} %bitcast.11, s32[32,4096]{1,0:T(8,128)} %bitcast.12, bf16[256,256]{1,0:T(8,128)(2,1)} %constant.56.clone.refs_4_, ...), custom_call_target="tpu_custom_call" | custom-call | tf_op jit(solution)/shard_map/filter/pallas_call | solution.py:196
  4.5 1.5 %collective-permute-start = (f32[16,48,128]{2,1,0:T(8,128)S(1)}, f32[16,48,128]{2,1,0:T(8,128)S(1)}, u32[]{:S(2)}, u32[]{:S(2)}) collective-permute-start(f32[16,48,128]{2,1,0:T(8,128)S(1)} %get-tuple-element.10), channel_id=1, source_target_pairs={{0,1},{1,0},{2,3},{3,2},{4,5},{5,4},{6,7},{7,6},{8,9},{9,8},{10,11... | collective-permute-start | bytes 1179656 | tf_op jit(solution)/shard_map/ppermute | solution.py:336
  6.0 0.0 copy-done.1
  6.0 0.1 iota_compare_fusion.1
  6.1 0.1 lt.36
  6.2 0.0 copy-done
  6.2 0.1 copy.11
  6.3 0.1 squeeze.19
  6.4 0.2 fusion.pick_ref
  6.6 0.7 %collective-permute-done.theirs = f32[16,48,128]{2,1,0:T(8,128)S(1)} collective-permute-done((f32[16,48,128]{2,1,0:T(8,128)S(1)}, f32[16,48,128]{2,1,0:T(8,128)S(1)}, u32[]{:S(2)}, u32[]{:S(2)}) %collective-permute-start) | collective-permute-done | bytes 393248 | tf_op jit(solution)/shard_map/ppermute | solution.py:336
  7.3 0.1 merge.1
  7.4 17.4 %all_to_all.10.r_ref = f32[16,64,128]{2,1,0:T(8,128)S(1)} all-to-all(f32[16,64,128]{2,1,0:T(8,128)S(1)} %merge.1), channel_id=1, replica_groups={{0,2,4,6,8,10,12,14,16,18,20,22,24,26,28,30},{1,3,5,7,9,11,13,15,17,19,..., dimensions={0} | all-to-all | bytes 1048576 | tf_op jit(solution)/shard_map/all_to_all | solution.py:341
  24.8 0.8 %collect.1 = f32[1024,128]{1,0:T(8,128)S(1)} custom-call(f32[16,64,128]{2,1,0:T(8,128)S(1)} %all_to_all.10.r_ref, bf16[1024,512]{1,0:T(8,128)(2,1)S(1)} %fusion.pick_ref), custom_call_target="tpu_custom_call" | custom-call | tf_op jit(solution)/shard_map/collect/pallas_call | solution.py:304
  25.6 21.4 %all_to_all.11 = f32[128,8,128]{2,1,0:T(8,128)S(1)} all-to-all(f32[128,8,128]{2,1,0:T(8,128)S(1)} %bitcast.7), channel_id=1, replica_groups=mesh['lev'=4,'strip'=32] {'lev','strip'}, dimensions={0} | all-to-all | bytes 1048576 | tf_op jit(solution)/shard_map/all_to_all | solution.py:343
  47.0 0.8 %copy.13 = f32[1024,128]{1,0:T(8,128)} copy(f32[1024,128]{1,0:T(8,128)S(1)} %bitcast.8) | data formatting | bytes 1048576
  (1 shorter events, 0.0 us)
Async XLA Ops:
  0.0 6.0 %copy-start.1 = (s32[1,128]{1,0:T(1,128)S(1)}, s32[1,128]{1,0:T(1,128)}, u32[]{:S(2)}) copy-start(s32[1,128]{1,0:T(1,128)} %param.15) | copy-start | bytes 1540
  0.0 6.2 %copy-start = (s32[1,128,8]{1,2,0:T(8,128)S(1)}, s32[1,128,8]{1,2,0:T(8,128)}, u32[]{:S(2)}) copy-start(s32[1,128,8]{1,2,0:T(8,128)} %param.14) | copy-start | bytes 12292
  4.5 2.9 %collective-permute-start = (f32[16,48,128]{2,1,0:T(8,128)S(1)}, f32[16,48,128]{2,1,0:T(8,128)S(1)}, u32[]{:S(2)}, u32[]{:S(2)}) collective-permute-start(f32[16,48,128]{2,1,0:T(8,128)S(1)} %get-tuple-element.10), channel_id=1, source_target_pairs={{0,1},{1,0},{2,3},{3,2},{4,5},{5,4},{6,7},{7,6},{8,9},{9,8},{10,11... | collective-permute-start | bytes 1179656 | tf_op jit(solution)/shard_map/ppermute | solution.py:336
